TPU v7x, 512 devices: a whole 4x8x8 slice. The times are simulated.
512 devices in a mesh: tp: 16 (over y_hi, z), sq: 8 (over x, core), sg: 4 (over y_lo).
Axes of the slice: x: 4, y: 8 (y_hi: 2, y_lo: 4; y = y_hi * 4 + y_lo), z: 8, core: 2. Of those that a mesh axis runs over, the one named last changes fastest.
Arguments:
- query: float32 [4, 1024, 4096], P('sg', 'sq', 'tp'), may hold values from -5 to 5
- key_in: float32 [4, 1024, 4096], P('sg', 'sq', 'tp'), may hold values from -5 to 5
- value: float32 [4, 1024, 4096], P('sg', 'sq', 'tp'), may hold values from -6 to 6
- out_grad: float32 [4, 1024, 4096], P('sg', 'sq', 'tp'), may hold values from -4 to 4
- w_out: float32 [4096, 4096], P(('sq', 'sg'), 'tp'), may hold values from -0.09375 to 0.09375
Outputs:
- query_grad: float32 [4, 1024, 4096], P('sg', 'sq', 'tp')
- key_grad: float32 [4, 1024, 4096], P('sg', 'sq', 'tp')
- value_grad: float32 [4, 1024, 4096], P('sg', 'sq', 'tp')
- w_out_grad: float32 [4096, 4096], P(('sq', 'sg'), 'tp')
All inputs are finite; a program needn't handle non-finite values.
Results may differ from a plain program's by a relative error of at most 0.00095.
Values sent between devices are 32-bit elements; how exact they have to be, the bound alone decides.
A program may use at most 64 MiB of HBM per device.

v0:
```python
import math

import jax
import jax.numpy as jnp
from jax import lax
from jax.sharding import PartitionSpec as P

HDIM = 128


def shifted(block, axis, distance):
    devices = range(lax.axis_size(axis))
    route = [((i - distance) % len(devices), i) for i in devices]
    return lax.ppermute(block, axis, route)


def shards(query, key_in, value, out_grad, w_out):
    highest = lax.Precision.HIGHEST
    scale_inv = 1.0 / math.sqrt(HDIM)
    tok_rows = query.shape[1]
    feat_width = query.shape[2]
    head_count = feat_width // HDIM
    queries = query[0]
    keys_own = key_in[0]
    values_own = value[0]
    out_full = lax.all_gather(out_grad[0], "tp", axis=1, tiled=True)
    keys_all, values_all = (
        lax.all_gather(keys_own, "sq", axis=0, tiled=True),
        lax.all_gather(values_own, "sq", axis=0, tiled=True),
    )
    key_count = keys_all.shape[0]
    q_heads = queries.reshape(tok_rows, head_count, HDIM)
    k_heads = keys_all.reshape(key_count, head_count, HDIM)
    v_heads = values_all.reshape(key_count, head_count, HDIM)
    scores = jnp.einsum("thd,shd->hts", q_heads, k_heads, precision=highest) * scale_inv
    row_top = jnp.max(scores, axis=2, keepdims=True)
    expos = jnp.exp(scores - row_top)
    row_sum = jnp.sum(expos, axis=2, keepdims=True)
    probs = expos / row_sum
    attended = jnp.einsum("hts,shd->thd", probs, v_heads, precision=highest)
    attended_flat = attended.reshape(tok_rows, feat_width)
    columns = out_full
    d_flat = jnp.dot(
        columns, lax.all_gather(w_out, ("sq", "sg"), axis=0, tiled=True), precision=highest
    )
    d_attended = d_flat.reshape(tok_rows, head_count, HDIM)
    columns = out_full
    w_grad = lax.psum_scatter(
        lax.dot_general(columns, attended_flat, (((0,), (0,)), ((), ())), precision=highest),
        ("sq", "sg"),
        scatter_dimension=0,
        tiled=True,
    )
    delta_rows = jnp.sum(d_attended * attended, axis=2).T
    d_probs = jnp.einsum("thd,shd->hts", d_attended, v_heads, precision=highest)
    d_scores = probs * (d_probs - delta_rows[:, :, None])
    grad_q = jnp.einsum("hts,shd->thd", d_scores, k_heads, precision=highest) * scale_inv
    group = lax.axis_size("sq")
    position = lax.axis_index("sq")

    def block_terms(block_idx):
        offset = block_idx * tok_rows
        score_part = lax.dynamic_slice_in_dim(d_scores, offset, tok_rows, 2)
        prob_part = lax.dynamic_slice_in_dim(probs, offset, tok_rows, 2)
        grad_k = jnp.einsum("hts,thd->shd", score_part, q_heads, precision=highest) * scale_inv
        grad_v = jnp.einsum("hts,thd->shd", prob_part, d_attended, precision=highest)
        return jnp.concatenate(
            [grad_k.reshape(tok_rows, feat_width), grad_v.reshape(tok_rows, feat_width)], axis=1
        )

    def cycle_step(index, carried):
        carried = carried + block_terms((position - index - 1) % group)
        return shifted(carried, "sq", 1)

    carried = lax.fori_loop(
        0, group - 1, cycle_step, jnp.zeros((tok_rows, 2 * feat_width), jnp.float32)
    )
    carried = carried + block_terms(position)
    grad_keys = carried[:, :feat_width]
    grad_values = carried[:, feat_width:]
    return (
        grad_q.reshape(1, tok_rows, feat_width),
        grad_keys.reshape(1, tok_rows, feat_width),
        grad_values.reshape(1, tok_rows, feat_width),
        w_grad,
    )


def solution(mesh):
    placed = (
        P("sg", "sq", "tp"),
        P("sg", "sq", "tp"),
        P("sg", "sq", "tp"),
        P("sg", "sq", "tp"),
        P(("sq", "sg"), "tp"),
    )
    return jax.shard_map(
        shards,
        mesh=mesh,
        in_specs=placed,
        out_specs=(
            P("sg", "sq", "tp"),
            P("sg", "sq", "tp"),
            P("sg", "sq", "tp"),
            P(("sq", "sg"), "tp"),
        ),
        check_vma=False,
    )
```

profile of v0, /device:TPU:1, one launch (start us, length us, event | category | flops | bytes accessed | tf_op | source)
XLA Modules:
  0.0 446.7 jit_solution(1311190272595154892)
XLA Ops:
  7.2 1.7 copy.23
  10.4 1.7 copy.26
  12.2 1.0 copy.22
  13.2 32.1 %all-gather.10.cloned.1.call-done = f32[1,1024,256]{1,2,0:T(8,128)} async-done(((f32[1,128,256]{1,2,0:T(8,128)}), f32[1,1024,256]{1,2,0:T(8,128)}) %all-gather.10.cloned.1.call-update) | async-done | bytes 1048592 | tf_op jit(solution)/shard_map/all_gather | solution.py:28
  45.3 2.4 fusion.17
  48.3 98.5 %all-gather.12.cloned.1.call-done = f32[1,128,4096]{2,1,0:T(8,128)} async-done(((f32[1,128,256]{2,1,0:T(8,128)}), f32[1,128,4096]{2,1,0:T(8,128)}) %all-gather.12.cloned.1.call-update) | async-done | bytes 2097168 | tf_op jit(solution)/shard_map/all_gather | solution.py:26
  146.7 95.6 %all-gather.8.cloned.1.call-done = f32[4096,256]{1,0:T(8,128)} async-done(((f32[128,256]{1,0:T(8,128)}), f32[4096,256]{1,0:T(8,128)}) %all-gather.8.cloned.1.call-update) | async-done | bytes 4194320 | tf_op jit(solution)/shard_map/all_gather | solution.py:44
  242.4 9.1 %fusion.6 = f32[128,256]{0,1:T(8,128)S(1)} fusion(f32[4096,256]{1,0:T(8,128)} %all-gather.8.cloned.1.call-done, f32[1,128,4096]{2,1,0:T(8,128)} %all-gather.12.cloned.1.call-done), kind=kOutput, calls=%fused_computation.9 | convolution fusion | flops 1610612736 | bytes 6422528 | tf_op jit(solution)/shard_map/dot_general | solution.py:43
  251.5 23.7 %all-gather.14.cloned.1.call-done = f32[1,1024,256]{1,2,0:T(8,128)} async-done(((f32[1,128,256]{1,2,0:T(8,128)}), f32[1,1024,256]{1,2,0:T(8,128)}) %all-gather.14.cloned.1.call-update) | async-done | bytes 1048592 | tf_op jit(solution)/shard_map/all_gather | solution.py:29
  275.2 2.4 fusion.11
  277.6 5.0 %convolution_bitcast_fusion = f32[4096,256]{0,1:T(8,128)} fusion(f32[128,256]{0,1:T(8,128)S(1)} %bitcast.71, f32[1,128,4096]{2,1,0:T(8,128)S(1)} %copy-done), kind=kOutput, calls=%fused_computation.7 | convolution fusion | flops 1610612736 | bytes 6422528 | tf_op jit(solution)/shard_map/dot_general | solution.py:49
  282.9 0.8 copy.33
  283.7 2.3 fusion.8
  286.0 1.1 convolution_multiply_fusion.3
  287.1 0.8 copy.35
  287.9 50.1 %while.15 = (s32[]{:T(128)}, f32[128,512]{0,1:T(8,128)S(1)}, s32[]{:T(128)}, f32[2,128,1024]{2,1,0:T(8,128)S(1)}, f32[128,2,128]{0,2,1:T(8,128)S(1)}, /*index=5*...) while((s32[]{:T(128)}, f32[128,512]{0,1:T(8,128)S(1)}, ...), condition=%wide.region_4.5_spmd, body=%wide.region_3.0_spmd.sunk | while | flops 100827152 | bytes 2621800 | solution.py:75
  288.6 0.8 collective-permute-start
  289.4 3.3 collective-permute-done
  293.3 2.5 collective-permute-start
  295.8 3.3 collective-permute-done
  299.7 2.5 collective-permute-start
  302.2 4.0 collective-permute-done
  306.8 2.5 collective-permute-start
  309.3 4.0 collective-permute-done
  313.9 2.5 collective-permute-start
  316.4 4.9 %collective-permute-done = f32[128,512]{0,1:T(8,128)S(1)} collective-permute-done((f32[128,512]{0,1:T(8,128)S(1)}, f32[128,512]{0,1:T(8,128)S(1)}, u32[]{:S(2)}, u32[]{:S(2)}) %collective-permute-start) | collective-permute-done | bytes 262176 | tf_op jit(solution)/shard_map/while/body/eval_jaxpr/ppermute | solution.py:14
  321.9 1.7 collective-permute-start
  323.6 6.2 %collective-permute-done = f32[128,512]{0,1:T(8,128)S(1)} collective-permute-done((f32[128,512]{0,1:T(8,128)S(1)}, f32[128,512]{0,1:T(8,128)S(1)}, u32[]{:S(2)}, u32[]{:S(2)}) %collective-permute-start) | collective-permute-done | bytes 262176 | tf_op jit(solution)/shard_map/while/body/eval_jaxpr/ppermute | solution.py:14
  330.7 7.4 %collective-permute-done = f32[128,512]{0,1:T(8,128)S(1)} collective-permute-done((f32[128,512]{0,1:T(8,128)S(1)}, f32[128,512]{0,1:T(8,128)S(1)}, u32[]{:S(2)}, u32[]{:S(2)}) %collective-permute-start) | collective-permute-done | bytes 262176 | tf_op jit(solution)/shard_map/while/body/eval_jaxpr/ppermute | solution.py:14
  338.6 0.7 slice_bitcast_fusion
  339.3 99.1 %reduce-scatter.2.cloned.1.call-done = f32[128,256]{0,1:T(8,128)} async-done(((f32[4096,256]{0,1:T(8,128)}), f32[128,256]{0,1:T(8,128)}) %reduce-scatter.2.cloned.1.call-update) | async-done | bytes 131088 | tf_op jit(solution)/shard_map/reduce_scatter | solution.py:48
  438.5 1.7 copy.36
  (50 shorter events, 7.6 us)
Async XLA Ops:
  7.2 38.1 %all-gather.10.cloned.1.call-start = ((), (), s32[]{:S(2)}) async-start(), calls=%async_computation.3 | async-start | bytes 1179648 | tf_op jit(solution)/shard_map/all_gather | solution.py:28
  8.9 137.9 %all-gather.12.cloned.1.call-start = ((), (), s32[]{:S(2)}) async-start(), calls=%async_computation.4 | async-start | bytes 2228224 | tf_op jit(solution)/shard_map/all_gather | solution.py:26
  9.6 232.7 %all-gather.8.cloned.1.call-start = ((), (), s32[]{:S(2)}) async-start(), calls=%async_computation.1 | async-start | bytes 4325376 | tf_op jit(solution)/shard_map/all_gather | solution.py:44
  10.4 264.8 %all-gather.14.cloned.1.call-start = ((), (), s32[]{:S(2)}) async-start(), calls=%async_computation.5 | async-start | bytes 1179648 | tf_op jit(solution)/shard_map/all_gather | solution.py:29
  12.1 426.4 %reduce-scatter.2.cloned.1.call-start = ((), (), s32[]{:S(2)}) async-start(), calls=%async_computation.2 | async-start | bytes 4325376 | tf_op jit(solution)/shard_map/reduce_scatter | solution.py:48
  13.2 34.5 %copy-start.1 = (f32[1,128,256]{1,2,0:T(8,128)}, f32[1,128,256]{1,2,0:T(8,128)S(1)}, u32[]{:S(2)}) copy-start(f32[1,128,256]{1,2,0:T(8,128)S(1)} %copy.22) | copy-start | bytes 393220
  251.5 26.1 %copy-start = (f32[1,128,4096]{2,1,0:T(8,128)S(1)}, f32[1,128,4096]{2,1,0:T(8,128)}, u32[]{:S(2)}) copy-start(f32[1,128,4096]{2,1,0:T(8,128)} %all-gather.12.cloned.1.call-done) | copy-start | bytes 6291460
  282.6 3.4 copy-start.3
  286.0 1.9 copy-start.2
  287.9 50.7 %copy-start.4 = (f32[128,256]{1,0:T(8,128)S(1)}, f32[128,256]{1,0:T(8,128)}, u32[]{:S(2)}) copy-start(f32[128,256]{1,0:T(8,128)} %copy.33) | copy-start | bytes 393220
  288.6 4.1 collective-permute-start
  293.3 5.8 %collective-permute-start = (f32[128,512]{0,1:T(8,128)S(1)}, f32[128,512]{0,1:T(8,128)S(1)}, u32[]{:S(2)}, u32[]{:S(2)}) collective-permute-start(f32[128,512]{0,1:T(8,128)S(1)} %maximum_add_fusion.3), channel_id=1, source_target_pairs={{28,0},{0,4},{4,8},{8,12},{12,16},{16,20},{20,24},{24,28},{29,1},{... | collective-permute-start | bytes 786440 | tf_op jit(solution)/shard_map/while/body/eval_jaxpr/ppermute | solution.py:14
  299.7 6.5 %collective-permute-start = (f32[128,512]{0,1:T(8,128)S(1)}, f32[128,512]{0,1:T(8,128)S(1)}, u32[]{:S(2)}, u32[]{:S(2)}) collective-permute-start(f32[128,512]{0,1:T(8,128)S(1)} %maximum_add_fusion.3), channel_id=1, source_target_pairs={{28,0},{0,4},{4,8},{8,12},{12,16},{16,20},{20,24},{24,28},{29,1},{... | collective-permute-start | bytes 786440 | tf_op jit(solution)/shard_map/while/body/eval_jaxpr/ppermute | solution.py:14
  306.8 6.4 %collective-permute-start = (f32[128,512]{0,1:T(8,128)S(1)}, f32[128,512]{0,1:T(8,128)S(1)}, u32[]{:S(2)}, u32[]{:S(2)}) collective-permute-start(f32[128,512]{0,1:T(8,128)S(1)} %maximum_add_fusion.3), channel_id=1, source_target_pairs={{28,0},{0,4},{4,8},{8,12},{12,16},{16,20},{20,24},{24,28},{29,1},{... | collective-permute-start | bytes 786440 | tf_op jit(solution)/shard_map/while/body/eval_jaxpr/ppermute | solution.py:14
  313.9 7.4 %collective-permute-start = (f32[128,512]{0,1:T(8,128)S(1)}, f32[128,512]{0,1:T(8,128)S(1)}, u32[]{:S(2)}, u32[]{:S(2)}) collective-permute-start(f32[128,512]{0,1:T(8,128)S(1)} %maximum_add_fusion.3), channel_id=1, source_target_pairs={{28,0},{0,4},{4,8},{8,12},{12,16},{16,20},{20,24},{24,28},{29,1},{... | collective-permute-start | bytes 786440 | tf_op jit(solution)/shard_map/while/body/eval_jaxpr/ppermute | solution.py:14
  321.9 7.9 %collective-permute-start = (f32[128,512]{0,1:T(8,128)S(1)}, f32[128,512]{0,1:T(8,128)S(1)}, u32[]{:S(2)}, u32[]{:S(2)}) collective-permute-start(f32[128,512]{0,1:T(8,128)S(1)} %maximum_add_fusion.3), channel_id=1, source_target_pairs={{28,0},{0,4},{4,8},{8,12},{12,16},{16,20},{20,24},{24,28},{29,1},{... | collective-permute-start | bytes 786440 | tf_op jit(solution)/shard_map/while/body/eval_jaxpr/ppermute | solution.py:14
  330.4 7.7 %collective-permute-start = (f32[128,512]{0,1:T(8,128)S(1)}, f32[128,512]{0,1:T(8,128)S(1)}, u32[]{:S(2)}, u32[]{:S(2)}) collective-permute-start(f32[128,512]{0,1:T(8,128)S(1)} %maximum_add_fusion.3), channel_id=1, source_target_pairs={{28,0},{0,4},{4,8},{8,12},{12,16},{16,20},{20,24},{24,28},{29,1},{... | collective-permute-start | bytes 786440 | tf_op jit(solution)/shard_map/while/body/eval_jaxpr/ppermute | solution.py:14
Sparse Core Ops, SparseCore 0:
  10.7 34.5 all-gather.9
  48.3 98.3 all-gather.11
  148.8 93.4 all-gather.7
  244.9 30.2 all-gather.13
  282.7 155.7 reduce-scatter.1
where the time goes:
time: 451 us; the launch traced here: 447 us
  waiting for transfers between devices  384 us (85%)
  matrix products  26.8 us (6%)
  between operations  13.9 us (3%)
  starting transfers between devices  12.9 us (3%)
  local copies, waits for them, and re-layouts  8.47 us (2%)
    reduce_scatter x1, waiting for transfers between devices, shards(): lax.psum_scatter(lax.dot_general(columns, attended_flat, (((0,), (0,)), (...  99.1 us
    all_gather x1, waiting for transfers between devices, shards(): out_full = lax.all_gather(out_grad[0], 'tp', axis=1, tiled=True)  98.5 us
    all_gather x1, waiting for transfers between devices, shards(): lax.all_gather(w_out, ('sq', 'sg'), axis=0, tiled=True)  95.6 us
    ppermute x7, waiting for transfers between devices, shifted(): return lax.ppermute(block, axis, route)  33.1 us
    all_gather x1, waiting for transfers between devices, shards(): lax.all_gather(keys_own, 'sq', axis=0, tiled=True)  32.1 us
    all_gather x1, waiting for transfers between devices, shards(): lax.all_gather(values_own, 'sq', axis=0, tiled=True)  23.7 us
    ppermute x7, starting transfers between devices, shifted(): return lax.ppermute(block, axis, route)  12.7 us
    dot_general x1, matrix products, shards(): jnp.dot(columns, lax.all_gather(w_out, ('sq', 'sg'), axis=0, tiled=True),...  9.1 us
  transfers between devices with their start and end apart: 12, of which 12 were waited for; matrix products, arithmetic and copies ran while one was open for 6% of the time, Pallas kernels for 0%

commit v1 on v0

v1 whole, which is shorter than its diff:
```python
import math

import jax
import jax.numpy as jnp
from jax import lax
from jax.experimental import pallas as pl
from jax.experimental.pallas import tpu as pltpu
from jax.sharding import PartitionSpec as P

HD = 128
F32 = jnp.float32
BF16 = jnp.bfloat16
NN = (((1,), (0,)), ((), ()))
NT = (((1,), (1,)), ((), ()))
TN = (((0,), (0,)), ((), ()))


def rcopy(src, dst, ssem, rsem, **dev):
    return pltpu.make_async_remote_copy(
        src_ref=src,
        dst_ref=dst,
        send_sem=ssem,
        recv_sem=rsem,
        device_id=dev,
        device_id_type=pl.DeviceIdType.MESH,
    )


def split(x):
    hi = x.astype(BF16)
    return hi, (x - hi.astype(F32)).astype(BF16)


def dot3(a, b, dims):
    d = lambda u, v: lax.dot_general(u, v, dims, preferred_element_type=F32)
    return d(a[0], b[0]) + (d(a[0], b[1]) + d(a[1], b[0]))


def body(
    q_ref, k_ref, v_ref, og_ref, w_ref,
    dq_ref, dk_ref, dv_ref, dw_ref,
    kvw, ogb, oghi, oglo, att, psend, dpart, part, sib, red, half, full,
    khi, klo, vhi, vlo, whi, wlo, pt, phi, plo,
    xs, xr, ss, sr, ys, yr, zs, zo, zr, ts, tr, ds, dr, rs1, rr1, rs2, rr2,
):
    t = lax.axis_index("tp")
    q = lax.axis_index("sq")
    s = lax.axis_index("sg")
    yh, z = lax.div(t, 8), lax.rem(t, 8)
    x, c = lax.div(q, 2), lax.rem(q, 2)
    par = lax.div(s, 2)
    odd = lax.rem(z + par, 2)
    ring = lambda d: yh * 8 + lax.rem(z + d + 8, 8)
    sq_at = lambda d: lax.rem(q + 2 * d + 8, 8)
    q_right, q_left, q_far, q_sib = sq_at(1), sq_at(-1), sq_at(2), x * 2 + 1 - c
    sibling = lambda b: b + 1 - 2 * c
    seg_at = lambda k: lax.rem(s + 1 + k, 4)

    barrier = pltpu.get_barrier_semaphore()
    partners = [{"sq": q_sib}, {"sq": q_right}, {"sq": q_left}, {"tp": ring(1)}, {"tp": ring(-1)}]
    for d in range(4):
        partners.append({"tp": (1 - yh) * 8 + z, "sg": lax.rem(s + d, 4)})
        if d > 0:
            partners.append({"sg": lax.rem(s + d, 4)})
    for p in partners:
        pl.semaphore_signal(barrier, inc=1, device_id=p, device_id_type=pl.DeviceIdType.MESH)
    pl.semaphore_wait(barrier, len(partners))

    sends = []

    def go(copy):
        copy.start()
        sends.append(copy)

    zi_own = lax.div(z, 2)
    ysend = []
    for h in range(2):
        target = 2 * lax.rem(z, 2) + h
        for y in range(2):
            mine = jnp.logical_and(yh == y, s == target)
            cp = rcopy(
                og_ref.at[:, pl.ds(h * HD, HD)],
                ogb.at[zi_own, s, yh],
                ys.at[h, y],
                yr.at[s, yh],
                tp=y * 8 + z,
                sg=target,
            )
            ysend.append((mine, cp))

            @pl.when(jnp.logical_not(mine))
            def _():
                cp.start()

            @pl.when(mine)
            def _():
                ogb[zi_own, s, yh] = og_ref[:, pl.ds(h * HD, HD)]

    ins = (k_ref, v_ref, w_ref)
    for a in range(3):
        go(rcopy(ins[a], kvw.at[a, q], xs.at[a, 0], xr.at[a, 0], sq=q_right))
        go(rcopy(ins[a], kvw.at[a, q], xs.at[a, 1], xr.at[a, 1], sq=q_left))
        go(rcopy(ins[a], kvw.at[a, q], ss.at[a, 0], sr.at[a, 0], sq=q_sib))
    for a in range(3):
        kvw[a, q] = ins[a][...]

    def near(a):
        rcopy(ins[a], kvw.at[a, q_left], xs.at[a, 0], xr.at[a, 0], sq=q_right).wait_recv()
        up = kvw.at[a, q_left, pl.ds(0, 64)]
        go(rcopy(up, up, xs.at[a, 2], xr.at[a, 2], sq=q_right))
        blk = kvw.at[a, q_left]
        go(rcopy(blk, blk, ss.at[a, 1], sr.at[a, 1], sq=q_sib))
        rcopy(ins[a], kvw.at[a, q_right], xs.at[a, 1], xr.at[a, 1], sq=q_left).wait_recv()
        low = kvw.at[a, q_right, pl.ds(64, 64)]
        go(rcopy(low, low, xs.at[a, 3], xr.at[a, 3], sq=q_left))
        blk = kvw.at[a, q_right]
        go(rcopy(blk, blk, ss.at[a, 2], sr.at[a, 2], sq=q_sib))

    def far(a):
        up = kvw.at[a, q_far, pl.ds(0, 64)]
        rcopy(up, up, xs.at[a, 2], xr.at[a, 2], sq=q_right).wait_recv()
        low = kvw.at[a, q_far, pl.ds(64, 64)]
        rcopy(low, low, xs.at[a, 3], xr.at[a, 3], sq=q_left).wait_recv()
        blk = kvw.at[a, q_far]
        go(rcopy(blk, blk, ss.at[a, 3], sr.at[a, 3], sq=q_sib))

    def siblings(a):
        for i, b in enumerate((q, q_left, q_right, q_far)):
            blk = kvw.at[a, sibling(b)]
            rcopy(blk, blk, ss.at[a, i], sr.at[a, i], sq=q_sib).wait_recv()

    def chunk(d, k):
        zi = lax.div(lax.rem(z - d + 16, 8), 2)
        return ogb.at[zi, seg_at(k)], zr.at[k, zi]

    def zcopy(d, k, sem, step):
        ref, rsem = chunk(d, k)
        return rcopy(ref, ref, sem, rsem, tp=ring(step))

    def own(k):
        @pl.when(odd == 0)
        def _():
            j = seg_at(k)
            for y in range(2):
                @pl.when(jnp.logical_not(jnp.logical_and(j == s, yh == y)))
                def _():
                    blk = ogb.at[zi_own, j, y]
                    rcopy(blk, blk, ys.at[0, y], yr.at[j, y], tp=t, sg=s).wait_recv()
            zcopy(0, k, zo.at[k, 0], 1).start()
            zcopy(0, k, zo.at[k, 1], -1).start()

    def pass_near(k):
        cp = zcopy(2 - odd, k, zs.at[k, 0], 1)
        cp.wait_recv()
        go(cp)
        cp = zcopy(6 + odd, k, zs.at[k, 1], -1)
        cp.wait_recv()
        go(cp)

    def pass_far(k):
        right_longer = k % 2 == 0
        cp = zcopy(4 - odd, k, zs.at[k, 2], 1 if right_longer else -1)
        cp.wait_recv()
        if right_longer:
            @pl.when(odd == 1)
            def _():
                cp.start()
                zcopy(5, k, zs.at[k, 2], -1).wait_recv()
        else:
            @pl.when(odd == 1)
            def _():
                cp2 = zcopy(5, k, zs.at[k, 2], -1)
                cp2.wait_recv()
                cp2.start()

    def partial_dot(k):
        j = seg_at(k)
        for zi in range(4):
            for y in range(2):
                hi, lo = split(ogb[zi, j, y])
                cols = pl.ds((y * 4 + zi) * HD, HD)
                oghi[j, :, cols] = hi
                oglo[j, :, cols] = lo
        res = dot3((oghi[j], oglo[j]), (whi[...], wlo[...]), NN)
        psend[k] = res
        if k < 3:
            go(rcopy(psend.at[k], dpart.at[k], ds.at[k], dr.at[k], sg=j))

    own(0)
    own(1)
    near(0)
    near(1)
    far(0)
    near(2)
    pass_near(0)
    own(2)
    far(1)
    far(2)
    pass_far(0)

    qs = q_ref[...] * (1.0 / math.sqrt(HD))
    qsp = [split(qs[:, h * HD:(h + 1) * HD]) for h in range(2)]
    siblings(0)
    for b in range(8):
        rows = pl.ds(b * 128, 128)
        khi[rows, :], klo[rows, :] = split(kvw[0, b])
    for h in range(2):
        cols = pl.ds(h * HD, HD)
        st = dot3((khi[:, cols], klo[:, cols]), qsp[h], NT)
        e = jnp.exp(st - jnp.max(st, axis=0, keepdims=True))
        p = e / jnp.sum(e, axis=0, keepdims=True)
        pt[h] = p
        phi[h], plo[h] = split(p)

    pass_near(1)
    own(3)
    siblings(1)
    for b in range(8):
        rows = pl.ds(b * 128, 128)
        vhi[rows, :], vlo[rows, :] = split(kvw[1, b])
    for h in range(2):
        cols = pl.ds(h * HD, HD)
        att[s, :, cols] = dot3((phi[h], plo[h]), (vhi[:, cols], vlo[:, cols]), TN)
    for k in range(3):
        go(rcopy(att.at[s], att.at[s], ts.at[k], tr.at[k], sg=seg_at(k)))
    pass_far(1)
    siblings(2)
    for b in range(8):
        rows = pl.ds(b * 128, 128)
        whi[rows, :], wlo[rows, :] = split(kvw[2, b])
    pass_near(2)
    partial_dot(0)
    partial_dot(1)
    pass_far(2)
    pass_near(3)
    partial_dot(2)
    pass_far(3)
    partial_dot(3)

    outs = (dk_ref, dv_ref, dw_ref)
    x_right, x_left, x_far = lax.rem(x + 1, 4), lax.rem(x + 3, 4), lax.rem(x + 2, 4)
    half_up, half_low = pl.ds(0, 64), pl.ds(64, 64)

    def put(a, val, cols):
        for b in range(8):
            part[a, b // 2, b % 2, :, cols] = val[b * 128:(b + 1) * 128]

    def sum_start(a):
        go(rcopy(part.at[a, :, 1 - c], sib.at[a], rs1.at[a], rr1.at[a], sq=q_sib))

    def sum_far(a):
        rcopy(part.at[a, :, 1 - c], sib.at[a], rs1.at[a], rr1.at[a], sq=q_sib).wait_recv()
        red[a, x_far] = part[a, x_far, c] + sib[a, x_far]
        up, low = red.at[a, x_far, half_up], red.at[a, x_far, half_low]
        go(rcopy(up, half.at[a, 0], rs2.at[a, 0], rr2.at[a, 0], sq=q_right))
        go(rcopy(low, half.at[a, 1], rs2.at[a, 1], rr2.at[a, 1], sq=q_left))
        red[a, x_right] = part[a, x_right, c] + sib[a, x_right]
        red[a, x_left] = part[a, x_left, c] + sib[a, x_left]
        red[a, x] = part[a, x, c] + sib[a, x]

    def sum_near(a):
        rcopy(half.at[a, 0], half.at[a, 0], rs2.at[a, 0], rr2.at[a, 0], sq=q_right).wait_recv()
        red[a, x_right, half_up] = red[a, x_right, half_up] + half[a, 0]
        go(rcopy(red.at[a, x_right], full.at[a, 0], rs2.at[a, 2], rr2.at[a, 2], sq=q_right))
        rcopy(half.at[a, 1], half.at[a, 1], rs2.at[a, 1], rr2.at[a, 1], sq=q_left).wait_recv()
        red[a, x_left, half_low] = red[a, x_left, half_low] + half[a, 1]
        go(rcopy(red.at[a, x_left], full.at[a, 1], rs2.at[a, 3], rr2.at[a, 3], sq=q_left))

    def sum_end(a):
        rcopy(full.at[a, 0], full.at[a, 0], rs2.at[a, 2], rr2.at[a, 2], sq=q_right).wait_recv()
        rcopy(full.at[a, 1], full.at[a, 1], rs2.at[a, 3], rr2.at[a, 3], sq=q_left).wait_recv()
        outs[a][...] = red[a, x] + (full[a, 0] + full[a, 1])

    for k in range(3):
        blk = att.at[lax.rem(s + 3 - k, 4)]
        rcopy(blk, blk, ts.at[k], tr.at[k], sg=seg_at(k)).wait_recv()
    asp = split(att[...].reshape(512, 256))
    dw = dot3((oghi[...].reshape(512, 1024), oglo[...].reshape(512, 1024)), asp, TN)
    put(2, dw, pl.ds(0, 256))
    sum_start(2)

    for k in range(3):
        rcopy(psend.at[k], dpart.at[k], ds.at[k], dr.at[k], sg=seg_at(k)).wait_recv()
    datt = (psend[3] + dpart[0]) + (dpart[1] + dpart[2])
    dsp = [split(datt[:, h * HD:(h + 1) * HD]) for h in range(2)]
    for h in range(2):
        put(1, dot3((phi[h], plo[h]), dsp[h], NN), pl.ds(h * HD, HD))
    sum_start(1)
    sum_far(2)
    ssp = []
    for h in range(2):
        cols = pl.ds(h * HD, HD)
        dp = dot3((vhi[:, cols], vlo[:, cols]), dsp[h], NT)
        p = pt[h]
        dsc = p * (dp - jnp.sum(p * dp, axis=0, keepdims=True))
        phi[h], plo[h] = split(dsc)
        put(0, dot3((phi[h], plo[h]), qsp[h], NN), cols)
    sum_start(0)
    sum_near(2)
    sum_far(1)
    sum_far(0)
    sum_near(1)
    sum_near(0)
    for h in range(2):
        cols = pl.ds(h * HD, HD)
        dq = dot3((phi[h], plo[h]), (khi[:, cols], klo[:, cols]), TN)
        dq_ref[:, cols] = dq * (1.0 / math.sqrt(HD))
    sum_end(2)
    sum_end(1)
    sum_end(0)

    for cp in sends:
        cp.wait_send()
    for mine, cp in ysend:
        @pl.when(jnp.logical_not(mine))
        def _():
            cp.wait_send()

    @pl.when(odd == 0)
    def _():
        for k in range(4):
            zcopy(0, k, zo.at[k, 0], 1).wait_send()
            zcopy(0, k, zo.at[k, 1], -1).wait_send()

    @pl.when(odd == 1)
    def _():
        for k in range(4):
            zcopy(3, k, zs.at[k, 2], 1).wait_send()


def shards(query, key_in, value, out_grad, w_out):
    blk = (128, 256)
    vmem = pl.BlockSpec(memory_space=pltpu.VMEM)
    sem = lambda *n: pltpu.SemaphoreType.DMA(n)
    outs = pl.pallas_call(
        body,
        out_shape=[jax.ShapeDtypeStruct(blk, F32)] * 4,
        in_specs=[vmem] * 5,
        out_specs=[vmem] * 4,
        scratch_shapes=[
            pltpu.VMEM((3, 8, 128, 256), F32),
            pltpu.VMEM((4, 4, 2, 128, 128), F32),
            pltpu.VMEM((4, 128, 1024), BF16),
            pltpu.VMEM((4, 128, 1024), BF16),
            pltpu.VMEM((4, 128, 256), F32),
            pltpu.VMEM((4, 128, 256), F32),
            pltpu.VMEM((3, 128, 256), F32),
            pltpu.VMEM((3, 4, 2, 128, 256), F32),
            pltpu.VMEM((3, 4, 128, 256), F32),
            pltpu.VMEM((3, 4, 128, 256), F32),
            pltpu.VMEM((3, 2, 64, 256), F32),
            pltpu.VMEM((3, 2, 128, 256), F32),
        ]
        + [pltpu.VMEM((1024, 256), BF16)] * 6
        + [
            pltpu.VMEM((2, 1024, 128), F32),
            pltpu.VMEM((2, 1024, 128), BF16),
            pltpu.VMEM((2, 1024, 128), BF16),
            sem(3, 4), sem(3, 4), sem(3, 4), sem(3, 4),
            sem(2, 2), sem(4, 2),
            sem(4, 3), sem(4, 2), sem(4, 4),
            sem(3), sem(3), sem(3), sem(3),
            sem(3), sem(3), sem(3, 4), sem(3, 4),
        ],
        compiler_params=pltpu.CompilerParams(
            collective_id=0, has_side_effects=True, vmem_limit_bytes=48 * 1024 * 1024
        ),
        cost_estimate=pl.CostEstimate(
            flops=3 * 940_000_000, bytes_accessed=1_200_000, transcendentals=262_144
        ),
    )(query[0], key_in[0], value[0], out_grad[0], w_out)
    dq, dk, dv, dw = outs
    return dq[None], dk[None], dv[None], dw


def solution(mesh):
    act = P("sg", "sq", "tp")
    wsp = P(("sq", "sg"), "tp")
    return jax.shard_map(
        shards,
        mesh=mesh,
        in_specs=(act, act, act, act, wsp),
        out_specs=(act, act, act, wsp),
        check_vma=False,
    )
```

time: 451 us -> 100 us (0.22)
  waiting for transfers between devices: 384 us -> 0 us
  Pallas kernels: 0 us -> 90.7 us
  matrix products: 26.8 us -> 0 us
  between operations: 13.9 us -> 0.65 us
  starting transfers between devices: 12.9 us -> 0 us
    all_gather x4 -> x0, waiting for transfers between devices: 250 us -> none  [the longest x1 98.5 us: shards(): out_full = lax.all_gather(out_grad[0], 'tp', axis=1, tiled=True)]
    reduce_scatter x1 -> x0, waiting for transfers between devices: 99.1 us -> none  [shards(): lax.psum_scatter(lax.dot_general(columns, attended_flat, (((0,), (0,)), (...]
    pallas_call x0 -> x1, Pallas kernels: none -> 90.7 us  [shards(): pl.pallas_call(body, out_shape=[jax.ShapeDtypeStruct(blk, F32)] * 4, in_s...]
    ppermute x7 -> x0, waiting for transfers between devices: 33.1 us -> none  [shifted(): return lax.ppermute(block, axis, route)]
    dot_general x22 -> x0, matrix products: 26.8 us -> none  [the longest x1 9.1 us: shards(): jnp.dot(columns, lax.all_gather(w_out, ('sq', 'sg'), axis=0, tiled=True),...]
    ppermute x7 -> x0, starting transfers between devices: 12.7 us -> none  [shifted(): return lax.ppermute(block, axis, route)]
  transfers between devices with their start and end apart: 12 -> 0, of which waited for: 12 -> 0; matrix products, arithmetic and copies ran while one was open for 6% -> 0% of each run, Pallas kernels for 0% -> 0%
where the time goes in v1:
time: 100 us; the launch traced here: 98.5 us
  Pallas kernels  90.7 us (91%)
  local copies, waits for them, and re-layouts  7.13 us (7%)
    pallas_call x1, Pallas kernels, shards(): pl.pallas_call(body, out_shape=[jax.ShapeDtypeStruct(blk, F32)] * 4, in_s...  90.7 us
    unnamed x14, local copies, waits for them, and re-layouts  7.13 us

profile of v1, /device:TPU:1, one launch (start us, length us, event | category | flops | bytes accessed | tf_op | source)
XLA Modules:
  0.0 98.5 jit_solution(6174271126631716102)
XLA Ops:
  0.6 0.0 copy-start
  0.6 0.9 copy-done
  1.5 0.0 copy-start.1
  1.5 0.9 copy-done.1
  2.4 0.0 copy-start.2
  2.4 0.9 copy-done.2
  3.3 0.0 copy-start.3
  3.3 0.9 copy-done.3
  4.3 0.0 copy-start.4
  4.3 0.9 copy-done.4
  5.2 90.7 %shard_map.84 = (f32[128,256]{1,0:T(8,128)S(1)}, f32[128,256]{1,0:T(8,128)S(1)}, f32[128,256]{1,0:T(8,128)S(1)}, f32[128,256]{1,0:T(8,128)S(1)}) custom-call(f32[128,256]{1,0:T(8,128)S(1)} %bitcast.10, f32[128,256]{1,0:T(8,128)S(1)} %bitcast.11, f32[128,256]{1,0:T(8,128)S(1)} %bitcast.12, f32[128,256]{1,0:T(8,128)S(1)} %bitcast.13, f32[128,256]{1,0:T(8,128)S(1)} %copy-done.4), custom_call_target="tpu_custom_call" | custom-call | flops 2820000000 | bytes 1200000 | tf_op jit(solution)/shard_map/pallas_call | solution.py:335
  95.9 0.7 copy.13
  96.6 0.7 copy.14
  97.2 0.7 copy.15
  97.9 0.7 copy.16
Async XLA Ops:
  0.6 0.9 copy-start
  1.5 0.9 copy-start.1
  2.4 0.9 copy-start.2
  3.3 0.9 copy-start.3
  4.3 0.9 copy-start.4

commit v2 on v0

v2 whole, which is shorter than its diff:
```python
import math

import jax
import jax.numpy as jnp
from jax import lax
from jax.experimental import pallas as pl
from jax.experimental.pallas import tpu as pltpu
from jax.sharding import PartitionSpec as P

HD = 128
F32 = jnp.float32
BF16 = jnp.bfloat16
NN = (((1,), (0,)), ((), ()))
NT = (((1,), (1,)), ((), ()))
TN = (((0,), (0,)), ((), ()))


def rcopy(src, dst, ssem, rsem, **dev):
    return pltpu.make_async_remote_copy(
        src_ref=src,
        dst_ref=dst,
        send_sem=ssem,
        recv_sem=rsem,
        device_id=dev,
        device_id_type=pl.DeviceIdType.MESH,
    )


def split(x):
    hi = x.astype(BF16)
    return hi, (x - hi.astype(F32)).astype(BF16)


def dot3(a, b, dims):
    d = lambda u, v: lax.dot_general(u, v, dims, preferred_element_type=F32)
    return d(a[0], b[0]) + (d(a[0], b[1]) + d(a[1], b[0]))


def body(
    q_ref, k_ref, v_ref, og_ref, w_ref,
    dq_ref, dk_ref, dv_ref, dw_ref,
    qh, kv, wb, ogb, oghi, oglo, att, ahi, alo, psend, dpart, dqs,
    wpart, wsib, wred, whalf, wfull, part, half, near_in, own_in,
    qhi, qlo, khi, klo, vhi, vlo, whi, wlo, pt, phi, plo,
    lin, qs_s, qs_r, kxs, kxr, kss, ksr, xs, xr, ss, sr, ys, yr, zs, zo, zr,
    ts, tr, ds, dr, ws1, wr1, ws2, wr2, hs, hr, fs, fr, os, orr, qos, qor,
):
    t = lax.axis_index("tp")
    q = lax.axis_index("sq")
    s = lax.axis_index("sg")
    yh, z = lax.div(t, 8), lax.rem(t, 8)
    x, c = lax.div(q, 2), lax.rem(q, 2)
    par = lax.div(s, 2)
    odd = lax.rem(z + par, 2)
    ring = lambda d: yh * 8 + lax.rem(z + d + 8, 8)
    x_right, x_left, x_far = lax.rem(x + 1, 4), lax.rem(x + 3, 4), lax.rem(x + 2, 4)
    q_right, q_left, q_far, q_sib = x_right * 2 + c, x_left * 2 + c, x_far * 2 + c, x * 2 + 1 - c
    sibling = lambda b: b + 1 - 2 * c
    seg_at = lambda k: lax.rem(s + 1 + k, 4)
    half_cols = lambda i: pl.ds(pl.multiple_of(i * HD, HD), HD)
    up, low = pl.ds(0, 64), pl.ds(64, 64)

    barrier = pltpu.get_barrier_semaphore()
    partners = []
    for d in range(4):
        partners.append({"tp": (1 - yh) * 8 + z, "sg": lax.rem(s + d, 4)})
        for core in range(2):
            if d > 0:
                partners.append({"sg": lax.rem(s + d, 4), "sq": x * 2 + core})
                if d != 2:
                    partners.append({"sq": lax.rem(x + d, 4) * 2 + core})
    partners += [{"tp": ring(1)}, {"tp": ring(-1)}, {"sq": q_sib}]
    for p in partners:
        pl.semaphore_signal(barrier, inc=1, device_id=p, device_id_type=pl.DeviceIdType.MESH)
    pl.semaphore_wait(barrier, len(partners))

    sends = []

    def go(copy):
        copy.start()
        sends.append(copy)

    zi_own = lax.div(z, 2)
    ysend = []
    for h in range(2):
        target = 2 * lax.rem(z, 2) + h
        nearer = jnp.where(jnp.abs(s - target) == 3, 1 - yh, yh)
        for i, y in enumerate((nearer, 1 - nearer)):
            mine = jnp.logical_and(yh == y, s == target)
            cp = rcopy(
                og_ref.at[:, pl.ds(h * HD, HD)],
                ogb.at[zi_own, s, yh],
                ys.at[h, i],
                yr.at[s, yh],
                tp=y * 8 + z,
                sg=target,
            )
            ysend.append((jnp.logical_not(mine), cp))
    for i in (0, 2):
        pl.when(ysend[i][0])(ysend[i][1].start)

    og_mine = og_ref.at[:, half_cols(lax.rem(s, 2))]
    og_local = pltpu.make_async_copy(og_mine, ogb.at[zi_own, s, yh], lin.at[4])

    nearer = [jnp.where(jnp.abs(seg_at(k) - s) == 3, 1 - yh, yh) for k in range(3)]
    pieces = [(s, yh)]
    pieces += [(seg_at(k), nearer[k]) for k in range(3)]
    pieces += [(seg_at(k), 1 - nearer[k]) for k in range(3)]
    pieces.append((s, 1 - yh))

    def zcopy(d, n, sem, step):
        zi = lax.div(lax.rem(z - d + 16, 8), 2)
        j, y = pieces[n]
        ref = ogb.at[zi, j, y]
        src = og_mine if d == 0 and n == 0 else ref
        return rcopy(src, ref, sem, zr.at[n, zi], tp=ring(step))

    def own(n):
        if n > 0:
            j, y = pieces[n]
            blk = ogb.at[zi_own, j, y]
            rcopy(blk, blk, ys.at[0, 0], yr.at[j, y], tp=t, sg=s).wait_recv()
        zcopy(0, n, zo.at[n, 0], 1).start()
        zcopy(0, n, zo.at[n, 1], -1).start()

    @pl.when(odd == 0)
    def _():
        own(0)
        og_local.start()

    kv_in = (k_ref, v_ref)
    for a in range(2):
        for side, xo in enumerate((x_right, x_left)):
            for core in range(2):
                go(rcopy(kv_in[a].at[:, pl.ds(core * HD, HD)], kv.at[a, q],
                         kxs.at[a, side, core], kxr.at[a, side, c], sq=xo * 2 + core))
        go(rcopy(kv_in[a].at[:, half_cols(1 - c)], kv.at[a, q], kss.at[a], ksr.at[a], sq=q_sib))
    go(rcopy(q_ref.at[:, half_cols(1 - c)], qh.at[c], qs_s, qs_r, sq=q_sib))
    go(rcopy(w_ref, wb.at[q], xs.at[0], xr.at[0], sq=q_right))
    go(rcopy(w_ref, wb.at[q], xs.at[1], xr.at[1], sq=q_left))
    go(rcopy(w_ref, wb.at[q], ss.at[0], sr.at[0], sq=q_sib))
    local = [pltpu.make_async_copy(kv_in[a].at[:, half_cols(c)], kv.at[a, q], lin.at[a]) for a in range(2)]
    local.append(pltpu.make_async_copy(w_ref, wb.at[q], lin.at[2]))
    local.append(pltpu.make_async_copy(q_ref.at[:, half_cols(c)], qh.at[c], lin.at[3]))
    for cp in local:
        cp.start()
    for i in (0, 2):
        pl.when(ysend[i][0])(ysend[i][1].wait_send)
        ysend[i + 1][1].start()

    def kv_copy(a, side, core, xs_, xd, rows=None, hop=0):
        blk = kv.at[a, xs_ * 2 + core]
        if rows is not None:
            blk = kv.at[a, xs_ * 2 + core, rows]
        return rcopy(blk, blk, kxs.at[a, side + 2 * hop, core], kxr.at[a, side + 2 * hop, core], sq=xd * 2 + c)

    def kv_near(a):
        for side, (xs_, xd, rows) in enumerate(((x_left, x_right, up), (x_right, x_left, low))):
            for core in range(2):
                kv_copy(a, side, core, xs_, xd).wait_recv()
                go(kv_copy(a, side, core, xs_, xd, rows, 1))

    def kv_done(a):
        for core in range(2):
            kv_copy(a, 0, core, x_far, x_right, up, 1).wait_recv()
            kv_copy(a, 1, core, x_far, x_left, low, 1).wait_recv()
        rcopy(kv.at[a, q_sib], kv.at[a, q_sib], kss.at[a], ksr.at[a], sq=q_sib).wait_recv()
        local[a].wait()

    def w_near():
        blk = wb.at[q_left]
        rcopy(blk, blk, xs.at[0], xr.at[0], sq=q_right).wait_recv()
        hb = wb.at[q_left, up]
        go(rcopy(hb, hb, xs.at[2], xr.at[2], sq=q_right))
        go(rcopy(blk, blk, ss.at[1], sr.at[1], sq=q_sib))
        blk = wb.at[q_right]
        rcopy(blk, blk, xs.at[1], xr.at[1], sq=q_left).wait_recv()
        hb = wb.at[q_right, low]
        go(rcopy(hb, hb, xs.at[3], xr.at[3], sq=q_left))
        go(rcopy(blk, blk, ss.at[2], sr.at[2], sq=q_sib))

    def w_far():
        for i, rows in enumerate((up, low)):
            hb = wb.at[q_far, rows]
            rcopy(hb, hb, xs.at[2 + i], xr.at[2 + i], sq=q_right).wait_recv()
        blk = wb.at[q_far]
        go(rcopy(blk, blk, ss.at[3], sr.at[3], sq=q_sib))

    def w_done():
        for i, b in enumerate((q, q_left, q_right, q_far)):
            blk = wb.at[sibling(b)]
            rcopy(blk, blk, ss.at[i], sr.at[i], sq=q_sib).wait_recv()
        local[2].wait()
        for b in range(8):
            rows = pl.ds(b * 128, 128)
            whi[rows, :], wlo[rows, :] = split(wb[b])

    def pass_near(n, odd):
        cp = zcopy(2 - odd, n, zs.at[n, 0], 1)
        cp.wait_recv()
        cp.start()
        cp = zcopy(6 + odd, n, zs.at[n, 1], -1)
        cp.wait_recv()
        cp.start()

    def pass_far(n):
        cp = zcopy(3, n, zs.at[n, 2], 1) if n % 2 == 0 else zcopy(5, n, zs.at[n, 2], -1)
        cp.wait_recv()
        cp.start()

    def ring_steps(owns=(), near_even=(), near_odd=(), fars=()):
        @pl.when(odd == 0)
        def _():
            for n in owns:
                own(n)
            for n in near_even:
                pass_near(n, 0)

        @pl.when(odd == 1)
        def _():
            for n in near_odd:
                pass_near(n, 1)
            for n in fars:
                pass_far(n)

    def arrived(n):
        @pl.when(odd == 0)
        def _():
            zcopy(4, n, zs.at[n, 2], 1).wait_recv()

        @pl.when(odd == 1)
        def _():
            zcopy(5 if n % 2 == 0 else 3, n, zs.at[n, 2], 1).wait_recv()

    def partial_dot(k):
        j = seg_at(k)
        for zi in range(4):
            for y in range(2):
                hi, lo = split(ogb[zi, j, y])
                cols = pl.ds((y * 4 + zi) * HD, HD)
                oghi[j, :, cols] = hi
                oglo[j, :, cols] = lo
        res = dot3((oghi[j], oglo[j]), (whi[...], wlo[...]), NN)
        psend[k, 0] = res[:, :HD]
        psend[k, 1] = res[:, HD:]
        if k < 3:
            for core in range(2):
                go(rcopy(psend.at[k, core], dpart.at[k, c], ds.at[k, core], dr.at[k, c], sg=j, sq=x * 2 + core))
        else:
            go(rcopy(psend.at[3, 1 - c], dpart.at[3, c], ds.at[3, 0], dr.at[3, c], sq=q_sib))
            dpart[3, c] = psend[3, c]

    def probs():
        rcopy(qh.at[1 - c], qh.at[1 - c], qs_s, qs_r, sq=q_sib).wait_recv()
        local[3].wait()
        qhi[...], qlo[...] = split(qh[...].reshape(256, HD) * (1.0 / math.sqrt(HD)))
        kv_done(0)
        khi[...], klo[...] = split(kv[0].reshape(1024, HD))
        st = dot3((khi[...], klo[...]), (qhi[...], qlo[...]), NT)
        e = jnp.exp(st - jnp.max(st, axis=0, keepdims=True))
        p = e / jnp.sum(e, axis=0, keepdims=True)
        pt[...] = p
        phi[...], plo[...] = split(p)

    tsends = []

    def to(copy):
        copy.start()
        tsends.append(copy)

    def attend():
        kv_done(1)
        vhi[...], vlo[...] = split(kv[1].reshape(1024, HD))
        res = dot3((phi[...], plo[...]), (vhi[...], vlo[...]), TN)
        dqs[...] = res.reshape(2, 128, HD)
        for k in range(3):
            for core in range(2):
                to(rcopy(dqs.at[core], att.at[s, c], ts.at[k, core], tr.at[k, c], sg=seg_at(k), sq=x * 2 + core))
        to(rcopy(dqs.at[1 - c], att.at[s, c], ts.at[3, 0], tr.at[3, c], sq=q_sib))
        att[s, c] = dqs[c]

    ring_steps(owns=(1,), near_odd=(0,))
    kv_near(0)
    ring_steps(owns=(2, 3), near_odd=(1,))
    kv_near(1)
    ring_steps(owns=(4,), near_even=(0,), near_odd=(2,))
    w_near()
    ring_steps(owns=(5, 6, 7), near_odd=(3,))
    probs()
    ring_steps(near_even=(1,), near_odd=(4,), fars=(0,))
    attend()
    ring_steps(near_even=(2,), near_odd=(5,), fars=(1,))
    w_far()
    ring_steps(near_even=(3,), near_odd=(6,))
    w_done()
    ring_steps(near_odd=(7,))
    ring_steps(near_even=(4,), fars=(2,))
    ring_steps(near_even=(5,), fars=(3,))
    ring_steps(near_even=(6,), fars=(4,))
    arrived(1)
    arrived(4)
    partial_dot(0)
    ring_steps(near_even=(7,), fars=(5,))
    arrived(2)
    arrived(5)
    partial_dot(1)
    ring_steps(fars=(6,))
    ring_steps(fars=(7,))
    arrived(3)
    arrived(6)
    partial_dot(2)

    @pl.when(odd == 0)
    def _():
        og_local.wait()

    arrived(0)
    arrived(7)
    partial_dot(3)

    for k in range(3):
        for head in range(2):
            blk = att.at[lax.rem(s + 3 - k, 4), head]
            rcopy(blk, blk, ts.at[k, 0], tr.at[k, head], sq=q_sib).wait_recv()
    blk = att.at[s, 1 - c]
    rcopy(blk, blk, ts.at[3, 0], tr.at[3, 1 - c], sq=q_sib).wait_recv()
    for head in range(2):
        cols = pl.ds(head * HD, HD)
        ahi[:, cols], alo[:, cols] = split(att[:, head].reshape(512, HD))
    dw = dot3(
        (oghi[...].reshape(512, 1024), oglo[...].reshape(512, 1024)), (ahi[...], alo[...]), TN
    )
    wpart[...] = dw.reshape(4, 2, 128, 256)
    go(rcopy(wpart.at[:, 1 - c], wsib, ws1, wr1, sq=q_sib))

    def dw_far():
        rcopy(wpart.at[:, 1 - c], wsib, ws1, wr1, sq=q_sib).wait_recv()
        wred[x_far] = wpart[x_far, c] + wsib[x_far]
        go(rcopy(wred.at[x_far, up], whalf.at[0], ws2.at[0], wr2.at[0], sq=q_right))
        go(rcopy(wred.at[x_far, low], whalf.at[1], ws2.at[1], wr2.at[1], sq=q_left))
        wred[x_right] = wpart[x_right, c] + wsib[x_right]
        go(rcopy(wred.at[x_right, low], wfull.at[0, low], ws2.at[2], wr2.at[2], sq=q_right))
        wred[x_left] = wpart[x_left, c] + wsib[x_left]
        go(rcopy(wred.at[x_left, up], wfull.at[1, up], ws2.at[3], wr2.at[3], sq=q_left))
        wred[x] = wpart[x, c] + wsib[x]

    def dw_near():
        rcopy(whalf.at[0], whalf.at[0], ws2.at[0], wr2.at[0], sq=q_right).wait_recv()
        wred[x_right, up] = wred[x_right, up] + whalf[0]
        go(rcopy(wred.at[x_right, up], wfull.at[0, up], ws2.at[4], wr2.at[4], sq=q_right))
        rcopy(whalf.at[1], whalf.at[1], ws2.at[1], wr2.at[1], sq=q_left).wait_recv()
        wred[x_left, low] = wred[x_left, low] + whalf[1]
        go(rcopy(wred.at[x_left, low], wfull.at[1, low], ws2.at[5], wr2.at[5], sq=q_left))

    def dw_end():
        for i, (side, rows) in enumerate(((0, low), (1, up), (0, up), (1, low))):
            blk = wfull.at[side, rows]
            rcopy(blk, blk, ws2.at[2 + i], wr2.at[2 + i], sq=q_right).wait_recv()
        dw_ref[...] = wred[x] + (wfull[0] + wfull[1])

    def near_rows(a, side, stage, xd, rows):
        for core in range(2):
            go(rcopy(part.at[a, xd, core, rows], near_in.at[a, side, c, rows],
                     fs.at[a, side, stage, core], fr.at[a, side, stage, c], sq=xd * 2 + core))

    def sum_start(a, val):
        part[a] = val.reshape(4, 2, 128, HD)
        go(rcopy(part.at[a, x_far, :, up], half.at[a, 0], hs.at[a, 0], hr.at[a, 0], sq=q_right))
        go(rcopy(part.at[a, x_far, :, low], half.at[a, 1], hs.at[a, 1], hr.at[a, 1], sq=q_left))
        near_rows(a, 0, 0, x_right, low)
        near_rows(a, 1, 0, x_left, up)
        go(rcopy(part.at[a, x, 1 - c], own_in.at[a], os.at[a], orr.at[a], sq=q_sib))

    def sum_near(a):
        rcopy(half.at[a, 0], half.at[a, 0], hs.at[a, 0], hr.at[a, 0], sq=q_right).wait_recv()
        part[a, x_right, :, up] = part[a, x_right, :, up] + half[a, 0]
        near_rows(a, 0, 1, x_right, up)
        rcopy(half.at[a, 1], half.at[a, 1], hs.at[a, 1], hr.at[a, 1], sq=q_left).wait_recv()
        part[a, x_left, :, low] = part[a, x_left, :, low] + half[a, 1]
        near_rows(a, 1, 1, x_left, low)

    outs = (dk_ref, dv_ref)

    def sum_end(a):
        for side in range(2):
            for stage in range(2):
                rows = low if side == stage else up
                for core in range(2):
                    blk = near_in.at[a, side, core, rows]
                    rcopy(blk, blk, fs.at[a, side, stage, core], fr.at[a, side, stage, core], sq=q_right).wait_recv()
        rcopy(own_in.at[a], own_in.at[a], os.at[a], orr.at[a], sq=q_sib).wait_recv()
        outs[a][:, half_cols(c)] = part[a, x, c] + (near_in[a, 0, c] + near_in[a, 1, c])
        outs[a][:, half_cols(1 - c)] = own_in[a] + (near_in[a, 0, 1 - c] + near_in[a, 1, 1 - c])

    dw_far()
    for k in range(3):
        for core in range(2):
            blk = dpart.at[k, core]
            rcopy(blk, blk, ds.at[k, 0], dr.at[k, core], sq=q_sib).wait_recv()
    blk = dpart.at[3, 1 - c]
    rcopy(blk, blk, ds.at[3, 0], dr.at[3, 1 - c], sq=q_sib).wait_recv()
    datt = ((dpart[0] + dpart[1]) + (dpart[2] + dpart[3])).reshape(256, HD)
    dsp = split(datt)
    sum_start(1, dot3((phi[...], plo[...]), dsp, NN))
    dp = dot3((vhi[...], vlo[...]), dsp, NT)
    p = pt[...]
    dsc = p * (dp - jnp.sum(p * dp, axis=0, keepdims=True))
    phi[...], plo[...] = split(dsc)
    sum_start(0, dot3((phi[...], plo[...]), (qhi[...], qlo[...]), NN))
    dw_near()
    sum_near(1)
    sum_near(0)
    for cp in tsends:
        cp.wait_send()
    dq = dot3((phi[...], plo[...]), (khi[...], klo[...]), TN) * (1.0 / math.sqrt(HD))
    dqs[...] = dq.reshape(2, 128, HD)
    go(rcopy(dqs.at[1 - c], dq_ref.at[:, half_cols(c)], qos, qor, sq=q_sib))
    dq_ref[:, half_cols(c)] = dqs[c]
    dw_end()
    sum_end(1)
    sum_end(0)
    rcopy(dqs.at[1 - c], dq_ref.at[:, half_cols(1 - c)], qos, qor, sq=q_sib).wait_recv()

    for cp in sends:
        cp.wait_send()
    for i in (1, 3):
        ysend[i][1].wait_send()

    @pl.when(odd == 0)
    def _():
        for n in range(8):
            zcopy(0, n, zo.at[n, 0], 1).wait_send()
            zcopy(0, n, zo.at[n, 1], -1).wait_send()

    @pl.when(odd == 1)
    def _():
        for n in range(8):
            zcopy(3, n, zs.at[n, 2], 1).wait_send()

    for n in range(8):
        for i in range(2):
            zcopy(3, n, zs.at[n, i], 1).wait_send()


def shards(query, key_in, value, out_grad, w_out):
    blk = (128, 256)
    vmem = pl.BlockSpec(memory_space=pltpu.VMEM)
    hbm = pl.BlockSpec(memory_space=pl.ANY)
    sem = lambda *n: pltpu.SemaphoreType.DMA(n)
    one = pltpu.SemaphoreType.DMA
    f32 = lambda *n: pltpu.VMEM(n, F32)
    b16 = lambda *n: pltpu.VMEM(n, BF16)
    outs = pl.pallas_call(
        body,
        out_shape=[jax.ShapeDtypeStruct(blk, F32)] * 4,
        in_specs=[hbm] * 5,
        out_specs=[vmem] * 4,
        scratch_shapes=[
            f32(2, 128, 128),
            f32(2, 8, 128, 128),
            f32(8, 128, 256),
            f32(4, 4, 2, 128, 128),
            b16(4, 128, 1024), b16(4, 128, 1024),
            f32(4, 2, 128, 128),
            b16(512, 256), b16(512, 256),
            f32(4, 2, 128, 128),
            f32(4, 2, 128, 128),
            f32(2, 128, 128),
            f32(4, 2, 128, 256),
            f32(4, 128, 256),
            f32(4, 128, 256),
            f32(2, 64, 256),
            f32(2, 128, 256),
            f32(2, 4, 2, 128, 128),
            f32(2, 2, 2, 64, 128),
            f32(2, 2, 2, 128, 128),
            f32(2, 128, 128),
            b16(256, 128), b16(256, 128),
            b16(1024, 128), b16(1024, 128),
            b16(1024, 128), b16(1024, 128),
            b16(1024, 256), b16(1024, 256),
            f32(1024, 256),
            b16(1024, 256), b16(1024, 256),
            sem(5), one, one,
            sem(2, 4, 2), sem(2, 4, 2), sem(2), sem(2),
            sem(4), sem(4), sem(4), sem(4),
            sem(2, 2), sem(4, 2),
            sem(8, 3), sem(8, 2), sem(8, 4),
            sem(4, 2), sem(4, 2), sem(4, 2), sem(4, 2),
            one, one, sem(6), sem(6),
            sem(2, 2), sem(2, 2),
            sem(2, 2, 2, 2), sem(2, 2, 2, 2),
            sem(2), sem(2), one, one,
        ],
        compiler_params=pltpu.CompilerParams(
            collective_id=0, has_side_effects=True, vmem_limit_bytes=60 * 1024 * 1024
        ),
        cost_estimate=pl.CostEstimate(
            flops=3 * 940_000_000, bytes_accessed=1_200_000, transcendentals=262_144
        ),
    )(query[0], key_in[0], value[0], out_grad[0], w_out)
    dq, dk, dv, dw = outs
    return dq[None], dk[None], dv[None], dw


def solution(mesh):
    act = P("sg", "sq", "tp")
    wsp = P(("sq", "sg"), "tp")
    return jax.shard_map(
        shards,
        mesh=mesh,
        in_specs=(act, act, act, act, wsp),
        out_specs=(act, act, act, wsp),
        check_vma=False,
    )
```

time: 451 us -> 80.1 us (0.18)
  the two profiles are of different devices: /device:TPU:1 before, /device:TPU:57 now
where the time goes in v2:
time: 80.1 us; the launch traced here: 79.9 us
  Pallas kernels  75.1 us (94%)
  local copies, waits for them, and re-layouts  4.16 us (5%)
    pallas_call x1, Pallas kernels, shards(): pl.pallas_call(body, out_shape=[jax.ShapeDtypeStruct(blk, F32)] * 4, in_s...  75.1 us
    unnamed x10, local copies, waits for them, and re-layouts  4.16 us

profile of v2, /device:TPU:57, one launch (start us, length us, event | category | flops | bytes accessed | tf_op | source)
XLA Modules:
  0.0 79.9 jit_solution(11078024349344423189)
XLA Ops:
  0.6 75.1 %shard_map.84 = (f32[128,256]{1,0:T(8,128)}, f32[128,256]{1,0:T(8,128)}, f32[128,256]{1,0:T(8,128)}, f32[128,256]{1,0:T(8,128)}) custom-call(f32[128,256]{1,0:T(8,128)} %bitcast.10, f32[128,256]{1,0:T(8,128)} %bitcast.11, f32[128,256]{1,0:T(8,128)} %bitcast.12, f32[128,256]{1,0:T(8,128)} %bitcast.13, f32[128,256]{1,0:T(8,128)} %w_ref.1), custom_call_target="tpu_custom_call" | custom-call | flops 2820000000 | bytes 1200000 | tf_op jit(solution)/shard_map/pallas_call | solution.py:453
  75.7 0.0 copy-start.2
  75.8 1.6 %copy.13 = f32[1,128,256]{2,1,0:T(8,128)} copy(f32[1,128,256]{2,1,0:T(8,128)} %bitcast.9) | data formatting | bytes 262144
  77.4 0.0 copy-done.2
  77.4 0.0 copy-start.1
  77.4 0.7 copy.14
  78.0 0.3 copy-done.1
  78.3 0.0 copy-start
  78.3 0.7 copy.15
  79.0 0.3 copy-done
  79.3 0.7 copy.16
Async XLA Ops:
  75.7 1.6 %copy-start.2 = (f32[128,256]{1,0:T(8,128)S(1)}, f32[128,256]{1,0:T(8,128)}, u32[]{:S(2)}) copy-start(f32[128,256]{1,0:T(8,128)} %get-tuple-element.9) | copy-start | bytes 393220
  77.4 1.0 %copy-start.1 = (f32[128,256]{1,0:T(8,128)S(1)}, f32[128,256]{1,0:T(8,128)}, u32[]{:S(2)}) copy-start(f32[128,256]{1,0:T(8,128)} %get-tuple-element.10) | copy-start | bytes 393220
  78.3 1.0 %copy-start = (f32[128,256]{1,0:T(8,128)S(1)}, f32[128,256]{1,0:T(8,128)}, u32[]{:S(2)}) copy-start(f32[128,256]{1,0:T(8,128)} %get-tuple-element.19) | copy-start | bytes 393220

commit v3 on v2

--- a/solution.py
+++ b/solution.py
@@ -43,7 +43,7 @@
     wpart, wsib, wred, whalf, wfull, part, half, near_in, own_in,
     qhi, qlo, khi, klo, vhi, vlo, whi, wlo, pt, phi, plo,
     lin, qs_s, qs_r, kxs, kxr, kss, ksr, xs, xr, ss, sr, ys, yr, zs, zo, zr,
-    ts, tr, ds, dr, ws1, wr1, ws2, wr2, hs, hr, fs, fr, os, orr, qos, qor,
+    ts, tr, tf_s, tf_r, ds, dr, ws1, wr1, ws2, wr2, hs, hr, fs, fr, os, orr, qos, qor,
 ):
     t = lax.axis_index("tp")
     q = lax.axis_index("sq")
@@ -56,9 +56,10 @@
     x_right, x_left, x_far = lax.rem(x + 1, 4), lax.rem(x + 3, 4), lax.rem(x + 2, 4)
     q_right, q_left, q_far, q_sib = x_right * 2 + c, x_left * 2 + c, x_far * 2 + c, x * 2 + 1 - c
     sibling = lambda b: b + 1 - 2 * c
-    seg_at = lambda k: lax.rem(s + 1 + k, 4)
+    seg_at = lambda k: lax.rem(s + (2, 1, 3, 4)[k], 4)
     half_cols = lambda i: pl.ds(pl.multiple_of(i * HD, HD), HD)
     up, low = pl.ds(0, 64), pl.ds(64, 64)
+    wup, wlow = pl.ds(0, 128), pl.ds(128, 128)
 
     barrier = pltpu.get_barrier_semaphore()
     partners = []
@@ -82,30 +83,33 @@
 
     zi_own = lax.div(z, 2)
     ysend = []
-    for h in range(2):
+    first = jnp.where(lax.rem(s - 2 * lax.rem(z, 2) + 7, 4) < 2, 0, 1)
+    for i, h in enumerate((first, 1 - first)):
         target = 2 * lax.rem(z, 2) + h
         nearer = jnp.where(jnp.abs(s - target) == 3, 1 - yh, yh)
-        for i, y in enumerate((nearer, 1 - nearer)):
-            mine = jnp.logical_and(yh == y, s == target)
+        for y in (nearer, 1 - nearer):
             cp = rcopy(
-                og_ref.at[:, pl.ds(h * HD, HD)],
+                og_ref.at[:, half_cols(h)],
                 ogb.at[zi_own, s, yh],
-                ys.at[h, i],
+                ys.at[len(ysend)],
                 yr.at[s, yh],
                 tp=y * 8 + z,
                 sg=target,
             )
-            ysend.append((jnp.logical_not(mine), cp))
-    for i in (0, 2):
-        pl.when(ysend[i][0])(ysend[i][1].start)
+            ysend.append(cp)
+            if len(ysend) == 3:
+                other = jnp.logical_or(yh != y, s != target)
+                pl.when(other)(cp.start)
+            else:
+                cp.start()
 
     og_mine = og_ref.at[:, half_cols(lax.rem(s, 2))]
     og_local = pltpu.make_async_copy(og_mine, ogb.at[zi_own, s, yh], lin.at[4])
 
-    nearer = [jnp.where(jnp.abs(seg_at(k) - s) == 3, 1 - yh, yh) for k in range(3)]
     pieces = [(s, yh)]
-    pieces += [(seg_at(k), nearer[k]) for k in range(3)]
-    pieces += [(seg_at(k), 1 - nearer[k]) for k in range(3)]
+    for k in range(3):
+        nearer = jnp.where(jnp.abs(seg_at(k) - s) == 3, 1 - yh, yh)
+        pieces += [(seg_at(k), nearer), (seg_at(k), 1 - nearer)]
     pieces.append((s, 1 - yh))
 
     def zcopy(d, n, sem, step):
@@ -119,7 +123,7 @@
         if n > 0:
             j, y = pieces[n]
             blk = ogb.at[zi_own, j, y]
-            rcopy(blk, blk, ys.at[0, 0], yr.at[j, y], tp=t, sg=s).wait_recv()
+            rcopy(blk, blk, ys.at[0], yr.at[j, y], tp=t, sg=s).wait_recv()
         zcopy(0, n, zo.at[n, 0], 1).start()
         zcopy(0, n, zo.at[n, 1], -1).start()
 
@@ -136,17 +140,11 @@
                          kxs.at[a, side, core], kxr.at[a, side, c], sq=xo * 2 + core))
         go(rcopy(kv_in[a].at[:, half_cols(1 - c)], kv.at[a, q], kss.at[a], ksr.at[a], sq=q_sib))
     go(rcopy(q_ref.at[:, half_cols(1 - c)], qh.at[c], qs_s, qs_r, sq=q_sib))
-    go(rcopy(w_ref, wb.at[q], xs.at[0], xr.at[0], sq=q_right))
-    go(rcopy(w_ref, wb.at[q], xs.at[1], xr.at[1], sq=q_left))
-    go(rcopy(w_ref, wb.at[q], ss.at[0], sr.at[0], sq=q_sib))
     local = [pltpu.make_async_copy(kv_in[a].at[:, half_cols(c)], kv.at[a, q], lin.at[a]) for a in range(2)]
     local.append(pltpu.make_async_copy(w_ref, wb.at[q], lin.at[2]))
     local.append(pltpu.make_async_copy(q_ref.at[:, half_cols(c)], qh.at[c], lin.at[3]))
     for cp in local:
         cp.start()
-    for i in (0, 2):
-        pl.when(ysend[i][0])(ysend[i][1].wait_send)
-        ysend[i + 1][1].start()
 
     def kv_copy(a, side, core, xs_, xd, rows=None, hop=0):
         blk = kv.at[a, xs_ * 2 + core]
@@ -166,6 +164,11 @@
             kv_copy(a, 1, core, x_far, x_left, low, 1).wait_recv()
         rcopy(kv.at[a, q_sib], kv.at[a, q_sib], kss.at[a], ksr.at[a], sq=q_sib).wait_recv()
         local[a].wait()
+
+    def w_start():
+        go(rcopy(w_ref, wb.at[q], xs.at[0], xr.at[0], sq=q_right))
+        go(rcopy(w_ref, wb.at[q], xs.at[1], xr.at[1], sq=q_left))
+        go(rcopy(w_ref, wb.at[q], ss.at[0], sr.at[0], sq=q_sib))
 
     def w_near():
         blk = wb.at[q_left]
@@ -195,11 +198,14 @@
             rows = pl.ds(b * 128, 128)
             whi[rows, :], wlo[rows, :] = split(wb[b])
 
+    on_right, on_left = (0, 2, 4, 1, 6, 3, 5, 7), (1, 3, 0, 5, 2, 7, 4, 6)
+
     def pass_near(n, odd):
-        cp = zcopy(2 - odd, n, zs.at[n, 0], 1)
+        right, left = (n, n) if odd else (on_right[n], on_left[n])
+        cp = zcopy(2 - odd, right, zs.at[right, 0], 1)
         cp.wait_recv()
         cp.start()
-        cp = zcopy(6 + odd, n, zs.at[n, 1], -1)
+        cp = zcopy(6 + odd, left, zs.at[left, 1], -1)
         cp.wait_recv()
         cp.start()
 
@@ -238,9 +244,9 @@
             for y in range(2):
                 hi, lo = split(ogb[zi, j, y])
                 cols = pl.ds((y * 4 + zi) * HD, HD)
-                oghi[j, :, cols] = hi
-                oglo[j, :, cols] = lo
-        res = dot3((oghi[j], oglo[j]), (whi[...], wlo[...]), NN)
+                oghi[k, :, cols] = hi
+                oglo[k, :, cols] = lo
+        res = dot3((oghi[k], oglo[k]), (whi[...], wlo[...]), NN)
         psend[k, 0] = res[:, :HD]
         psend[k, 1] = res[:, HD:]
         if k < 3:
@@ -262,7 +268,21 @@
         pt[...] = p
         phi[...], plo[...] = split(p)
 
-    tsends = []
+    ends = (None, s == 3, s == 0)
+    inner = jnp.logical_and(s > 0, s < 3)
+    far_seg = jnp.where(s == 2, 0, 3)
+    tsends, tnear = [], []
+
+    def att_hop(j, to_seg):
+        return rcopy(att.at[j], att.at[j], tf_s, tf_r, sg=to_seg)
+
+    def att_forward():
+        @pl.when(inner)
+        def _():
+            for head in range(2):
+                blk = att.at[far_seg, head]
+                rcopy(blk, blk, ts.at[0, 0], tr.at[0, head], sq=q_sib).wait_recv()
+            att_hop(far_seg, 3 - far_seg).start()
 
     def to(copy):
         copy.start()
@@ -275,40 +295,78 @@
         dqs[...] = res.reshape(2, 128, HD)
         for k in range(3):
             for core in range(2):
-                to(rcopy(dqs.at[core], att.at[s, c], ts.at[k, core], tr.at[k, c], sg=seg_at(k), sq=x * 2 + core))
+                cp = rcopy(dqs.at[core], att.at[s, c], ts.at[k, core], tr.at[k, c], sg=seg_at(k), sq=x * 2 + core)
+                if k == 0:
+                    to(cp)
+                else:
+                    pl.when(jnp.logical_not(ends[k]))(cp.start)
+                    tnear.append((k, cp))
         to(rcopy(dqs.at[1 - c], att.at[s, c], ts.at[3, 0], tr.at[3, c], sq=q_sib))
         att[s, c] = dqs[c]
 
+    def att_pairs(k):
+        j = seg_at(k)
+        if k < 3:
+            k_from = (0, 2, 1)[k]
+
+            def direct():
+                for head in range(2):
+                    blk = att.at[j, head]
+                    rcopy(blk, blk, ts.at[k_from, 0], tr.at[k_from, head], sq=q_sib).wait_recv()
+
+            if k == 0:
+                pl.when(jnp.logical_not(inner))(direct)
+            else:
+                pl.when(jnp.logical_not(ends[k]))(direct)
+                pl.when(ends[k])(att_hop(j, s).wait_recv)
+        else:
+            blk = att.at[s, 1 - c]
+            rcopy(blk, blk, ts.at[3, 0], tr.at[3, 1 - c], sq=q_sib).wait_recv()
+        for head in range(2):
+            cols = pl.ds(head * HD, HD)
+            ahi[k, :, cols], alo[k, :, cols] = split(att[j, head])
+
+    def dw_add(k):
+        att_pairs(k)
+        att_pairs(k + 1)
+        rows = pl.ds(k, 2)
+        a = (ahi[rows].reshape(256, 256), alo[rows].reshape(256, 256))
+        g = (oghi[rows].reshape(256, 1024), oglo[rows].reshape(256, 1024))
+        dw = dot3(a, g, TN)
+        for b in range(8):
+            part_b = dw[:, b * 128:(b + 1) * 128]
+            wpart[b // 2, b % 2] = part_b if k == 0 else wpart[b // 2, b % 2] + part_b
+
     ring_steps(owns=(1,), near_odd=(0,))
     kv_near(0)
-    ring_steps(owns=(2, 3), near_odd=(1,))
+    ring_steps(owns=(2, 3, 4), near_odd=(1,))
     kv_near(1)
-    ring_steps(owns=(4,), near_even=(0,), near_odd=(2,))
+    w_start()
+    ring_steps(owns=(5, 6), near_odd=(2,))
+    probs()
+    ring_steps(owns=(7,), near_odd=(3, 4))
+    attend()
+    ring_steps(near_even=(0,), near_odd=(5,))
     w_near()
-    ring_steps(owns=(5, 6, 7), near_odd=(3,))
-    probs()
-    ring_steps(near_even=(1,), near_odd=(4,), fars=(0,))
-    attend()
-    ring_steps(near_even=(2,), near_odd=(5,), fars=(1,))
+    ring_steps(near_even=(1, 2, 3), near_odd=(6, 7))
     w_far()
-    ring_steps(near_even=(3,), near_odd=(6,))
+    ring_steps(near_even=(4,), fars=(0,))
     w_done()
-    ring_steps(near_odd=(7,))
-    ring_steps(near_even=(4,), fars=(2,))
-    ring_steps(near_even=(5,), fars=(3,))
-    ring_steps(near_even=(6,), fars=(4,))
+    ring_steps(near_even=(5, 6, 7), fars=(1, 2, 3))
+    att_forward()
+    ring_steps(fars=(4,))
     arrived(1)
+    arrived(2)
+    partial_dot(0)
+    ring_steps(fars=(5,))
+    arrived(3)
     arrived(4)
-    partial_dot(0)
-    ring_steps(near_even=(7,), fars=(5,))
-    arrived(2)
+    partial_dot(1)
+    ring_steps(fars=(6, 7))
     arrived(5)
-    partial_dot(1)
-    ring_steps(fars=(6,))
-    ring_steps(fars=(7,))
-    arrived(3)
     arrived(6)
     partial_dot(2)
+    dw_add(0)
 
     @pl.when(odd == 0)
     def _():
@@ -317,46 +375,33 @@
     arrived(0)
     arrived(7)
     partial_dot(3)
-
-    for k in range(3):
-        for head in range(2):
-            blk = att.at[lax.rem(s + 3 - k, 4), head]
-            rcopy(blk, blk, ts.at[k, 0], tr.at[k, head], sq=q_sib).wait_recv()
-    blk = att.at[s, 1 - c]
-    rcopy(blk, blk, ts.at[3, 0], tr.at[3, 1 - c], sq=q_sib).wait_recv()
-    for head in range(2):
-        cols = pl.ds(head * HD, HD)
-        ahi[:, cols], alo[:, cols] = split(att[:, head].reshape(512, HD))
-    dw = dot3(
-        (oghi[...].reshape(512, 1024), oglo[...].reshape(512, 1024)), (ahi[...], alo[...]), TN
-    )
-    wpart[...] = dw.reshape(4, 2, 128, 256)
+    dw_add(2)
     go(rcopy(wpart.at[:, 1 - c], wsib, ws1, wr1, sq=q_sib))
 
     def dw_far():
         rcopy(wpart.at[:, 1 - c], wsib, ws1, wr1, sq=q_sib).wait_recv()
         wred[x_far] = wpart[x_far, c] + wsib[x_far]
-        go(rcopy(wred.at[x_far, up], whalf.at[0], ws2.at[0], wr2.at[0], sq=q_right))
-        go(rcopy(wred.at[x_far, low], whalf.at[1], ws2.at[1], wr2.at[1], sq=q_left))
+        go(rcopy(wred.at[x_far, wup], whalf.at[0], ws2.at[0], wr2.at[0], sq=q_right))
+        go(rcopy(wred.at[x_far, wlow], whalf.at[1], ws2.at[1], wr2.at[1], sq=q_left))
         wred[x_right] = wpart[x_right, c] + wsib[x_right]
-        go(rcopy(wred.at[x_right, low], wfull.at[0, low], ws2.at[2], wr2.at[2], sq=q_right))
+        go(rcopy(wred.at[x_right, wlow], wfull.at[0, wlow], ws2.at[2], wr2.at[2], sq=q_right))
         wred[x_left] = wpart[x_left, c] + wsib[x_left]
-        go(rcopy(wred.at[x_left, up], wfull.at[1, up], ws2.at[3], wr2.at[3], sq=q_left))
+        go(rcopy(wred.at[x_left, wup], wfull.at[1, wup], ws2.at[3], wr2.at[3], sq=q_left))
         wred[x] = wpart[x, c] + wsib[x]
 
     def dw_near():
         rcopy(whalf.at[0], whalf.at[0], ws2.at[0], wr2.at[0], sq=q_right).wait_recv()
-        wred[x_right, up] = wred[x_right, up] + whalf[0]
-        go(rcopy(wred.at[x_right, up], wfull.at[0, up], ws2.at[4], wr2.at[4], sq=q_right))
+        wred[x_right, wup] = wred[x_right, wup] + whalf[0]
+        go(rcopy(wred.at[x_right, wup], wfull.at[0, wup], ws2.at[4], wr2.at[4], sq=q_right))
         rcopy(whalf.at[1], whalf.at[1], ws2.at[1], wr2.at[1], sq=q_left).wait_recv()
-        wred[x_left, low] = wred[x_left, low] + whalf[1]
-        go(rcopy(wred.at[x_left, low], wfull.at[1, low], ws2.at[5], wr2.at[5], sq=q_left))
+        wred[x_left, wlow] = wred[x_left, wlow] + whalf[1]
+        go(rcopy(wred.at[x_left, wlow], wfull.at[1, wlow], ws2.at[5], wr2.at[5], sq=q_left))
 
     def dw_end():
-        for i, (side, rows) in enumerate(((0, low), (1, up), (0, up), (1, low))):
+        for i, (side, rows) in enumerate(((0, wlow), (1, wup), (0, wup), (1, wlow))):
             blk = wfull.at[side, rows]
             rcopy(blk, blk, ws2.at[2 + i], wr2.at[2 + i], sq=q_right).wait_recv()
-        dw_ref[...] = wred[x] + (wfull[0] + wfull[1])
+        dw_ref[...] = (wred[x] + (wfull[0] + wfull[1])).T
 
     def near_rows(a, side, stage, xd, rows):
         for core in range(2):
@@ -409,13 +454,16 @@
     sum_start(0, dot3((phi[...], plo[...]), (qhi[...], qlo[...]), NN))
     dw_near()
     sum_near(1)
-    sum_near(0)
     for cp in tsends:
         cp.wait_send()
+    for k, cp in tnear:
+        pl.when(jnp.logical_not(ends[k]))(cp.wait_send)
+    pl.when(inner)(att_hop(far_seg, 3 - far_seg).wait_send)
     dq = dot3((phi[...], plo[...]), (khi[...], klo[...]), TN) * (1.0 / math.sqrt(HD))
     dqs[...] = dq.reshape(2, 128, HD)
     go(rcopy(dqs.at[1 - c], dq_ref.at[:, half_cols(c)], qos, qor, sq=q_sib))
     dq_ref[:, half_cols(c)] = dqs[c]
+    sum_near(0)
     dw_end()
     sum_end(1)
     sum_end(0)
@@ -423,8 +471,9 @@
 
     for cp in sends:
         cp.wait_send()
-    for i in (1, 3):
-        ysend[i][1].wait_send()
+    for i in (0, 1, 3):
+        ysend[i].wait_send()
+    pl.when(other)(ysend[2].wait_send)
 
     @pl.when(odd == 0)
     def _():
@@ -442,10 +491,19 @@
             zcopy(3, n, zs.at[n, i], 1).wait_send()
 
 
+def keep(*refs):
+    sems = refs[8]
+    copies = [pltpu.make_async_copy(refs[i], refs[4 + i], sems.at[i]) for i in range(4)]
+    for cp in copies:
+        cp.start()
+    for cp in copies:
+        cp.wait()
+
+
 def shards(query, key_in, value, out_grad, w_out):
     blk = (128, 256)
     vmem = pl.BlockSpec(memory_space=pltpu.VMEM)
-    hbm = pl.BlockSpec(memory_space=pl.ANY)
+    hbm = pl.BlockSpec(memory_space=pltpu.HBM)
     sem = lambda *n: pltpu.SemaphoreType.DMA(n)
     one = pltpu.SemaphoreType.DMA
     f32 = lambda *n: pltpu.VMEM(n, F32)
@@ -462,15 +520,15 @@
             f32(4, 4, 2, 128, 128),
             b16(4, 128, 1024), b16(4, 128, 1024),
             f32(4, 2, 128, 128),
-            b16(512, 256), b16(512, 256),
+            b16(4, 128, 256), b16(4, 128, 256),
             f32(4, 2, 128, 128),
             f32(4, 2, 128, 128),
             f32(2, 128, 128),
-            f32(4, 2, 128, 256),
-            f32(4, 128, 256),
-            f32(4, 128, 256),
-            f32(2, 64, 256),
-            f32(2, 128, 256),
+            f32(4, 2, 256, 128),
+            f32(4, 256, 128),
+            f32(4, 256, 128),
+            f32(2, 128, 128),
+            f32(2, 256, 128),
             f32(2, 4, 2, 128, 128),
             f32(2, 2, 2, 64, 128),
             f32(2, 2, 2, 128, 128),
@@ -484,9 +542,9 @@
             sem(5), one, one,
             sem(2, 4, 2), sem(2, 4, 2), sem(2), sem(2),
             sem(4), sem(4), sem(4), sem(4),
-            sem(2, 2), sem(4, 2),
+            sem(4), sem(4, 2),
             sem(8, 3), sem(8, 2), sem(8, 4),
-            sem(4, 2), sem(4, 2), sem(4, 2), sem(4, 2),
+            sem(4, 2), sem(4, 2), one, one, sem(4, 2), sem(4, 2),
             one, one, sem(6), sem(6),
             sem(2, 2), sem(2, 2),
             sem(2, 2, 2, 2), sem(2, 2, 2, 2),
@@ -499,7 +557,14 @@
             flops=3 * 940_000_000, bytes_accessed=1_200_000, transcendentals=262_144
         ),
     )(query[0], key_in[0], value[0], out_grad[0], w_out)
-    dq, dk, dv, dw = outs
+    dq, dk, dv, dw = pl.pallas_call(
+        keep,
+        out_shape=[jax.ShapeDtypeStruct(blk, F32)] * 4,
+        in_specs=[vmem] * 4,
+        out_specs=[hbm] * 4,
+        scratch_shapes=[sem(4)],
+        compiler_params=pltpu.CompilerParams(vmem_limit_bytes=60 * 1024 * 1024),
+    )(*outs)
     return dq[None], dk[None], dv[None], dw
 
 

time: 80.1 us -> 75.1 us (0.938)
  the two profiles are of different devices: /device:TPU:57 before, /device:TPU:1 now
where the time goes in v3:
time: 75.1 us; the launch traced here: 75 us
  Pallas kernels  74.3 us (99%)
    pallas_call x1, Pallas kernels, shards(): pl.pallas_call(body, out_shape=[jax.ShapeDtypeStruct(blk, F32)] * 4, in_s...  72.4 us
    pallas_call x1, Pallas kernels, shards(): pl.pallas_call(keep, out_shape=[jax.ShapeDtypeStruct(blk, F32)] * 4, in_s...  1.91 us

profile of v3, /device:TPU:1, one launch (start us, length us, event | category | flops | bytes accessed | tf_op | source)
XLA Modules:
  0.0 75.0 jit_solution(9622175520661416844)
XLA Ops:
  0.6 72.4 %shard_map.84 = (f32[128,256]{1,0:T(8,128)}, f32[128,256]{1,0:T(8,128)}, f32[128,256]{1,0:T(8,128)}, f32[128,256]{1,0:T(8,128)}) custom-call(f32[128,256]{1,0:T(8,128)} %bitcast.7, f32[128,256]{1,0:T(8,128)} %bitcast.8, f32[128,256]{1,0:T(8,128)} %bitcast.9, f32[128,256]{1,0:T(8,128)} %bitcast.10, f32[128,256]{1,0:T(8,128)} %w_ref.1), custom_call_target="tpu_custom_call" | custom-call | flops 2820000000 | bytes 1200000 | tf_op jit(solution)/shard_map/pallas_call | solution.py:511
  73.1 1.9 %shard_map.85 = (f32[128,256]{1,0:T(8,128)}, f32[128,256]{1,0:T(8,128)}, f32[128,256]{1,0:T(8,128)}, f32[128,256]{1,0:T(8,128)}) custom-call(f32[128,256]{1,0:T(8,128)} %get-tuple-element.12.refs_0_, f32[128,256]{1,0:T(8,128)} %get-tuple-element.13.refs_1_, f32[128,256]{1,0:T(8,128)} %get-tuple-element.14.refs_2_, f32[128,256]{1,0:T(8,128)} %get-tuple-element.15.refs_3_), custom_call_target="tpu_custom_call" | custom-call | tf_op jit(solution)/shard_map/pallas_call | solution.py:560

commit v4 on v3

--- a/solution.py
+++ b/solution.py
@@ -39,11 +39,11 @@
 def body(
     q_ref, k_ref, v_ref, og_ref, w_ref,
     dq_ref, dk_ref, dv_ref, dw_ref,
-    qh, kv, wb, ogb, oghi, oglo, att, ahi, alo, psend, dpart, dqs,
+    qh, kv, wb, ogb, oghi, oglo, att, ahi, alo, psend, dpart, relayed, dqs,
     wpart, wsib, wred, whalf, wfull, part, half, near_in, own_in,
     qhi, qlo, khi, klo, vhi, vlo, whi, wlo, pt, phi, plo,
     lin, qs_s, qs_r, kxs, kxr, kss, ksr, xs, xr, ss, sr, ys, yr, zs, zo, zr,
-    ts, tr, tf_s, tf_r, ds, dr, ws1, wr1, ws2, wr2, hs, hr, fs, fr, os, orr, qos, qor,
+    ts, tr, tf_s, tf_r, ds, dr, rel_r, ws1, wr1, ws2, wr2, hs, hr, fs, fr, os, orr, qos, qor,
 ):
     t = lax.axis_index("tp")
     q = lax.axis_index("sq")
@@ -56,7 +56,15 @@
     x_right, x_left, x_far = lax.rem(x + 1, 4), lax.rem(x + 3, 4), lax.rem(x + 2, 4)
     q_right, q_left, q_far, q_sib = x_right * 2 + c, x_left * 2 + c, x_far * 2 + c, x * 2 + 1 - c
     sibling = lambda b: b + 1 - 2 * c
-    seg_at = lambda k: lax.rem(s + (2, 1, 3, 4)[k], 4)
+    att_seg = lambda k: lax.rem(s + (2, 1, 3)[k], 4)
+    inner = jnp.logical_and(s > 0, s < 3)
+    order = (
+        jnp.where(inner, lax.rem(s + 1, 4), 3 - s),
+        jnp.where(inner, lax.rem(s + 3, 4), lax.rem(s + 2, 4)),
+        jnp.where(inner, lax.rem(s + 2, 4), jnp.where(s == 0, 1, 2)),
+        s,
+    )
+    seg_at = lambda k: order[k]
     half_cols = lambda i: pl.ds(pl.multiple_of(i * HD, HD), HD)
     up, low = pl.ds(0, 64), pl.ds(64, 64)
     wup, wlow = pl.ds(0, 128), pl.ds(128, 128)
@@ -82,35 +90,37 @@
         sends.append(copy)
 
     zi_own = lax.div(z, 2)
-    ysend = []
-    first = jnp.where(lax.rem(s - 2 * lax.rem(z, 2) + 7, 4) < 2, 0, 1)
-    for i, h in enumerate((first, 1 - first)):
+    in_pair = lax.rem(z, 2) == par
+    next_to = 1 - lax.rem(s, 2)
+
+    def y_send(i, h, far):
         target = 2 * lax.rem(z, 2) + h
-        nearer = jnp.where(jnp.abs(s - target) == 3, 1 - yh, yh)
-        for y in (nearer, 1 - nearer):
-            cp = rcopy(
-                og_ref.at[:, half_cols(h)],
-                ogb.at[zi_own, s, yh],
-                ys.at[len(ysend)],
-                yr.at[s, yh],
-                tp=y * 8 + z,
-                sg=target,
-            )
-            ysend.append(cp)
-            if len(ysend) == 3:
-                other = jnp.logical_or(yh != y, s != target)
-                pl.when(other)(cp.start)
-            else:
-                cp.start()
+        y = jnp.where(jnp.abs(s - target) == 3, 1 - yh, yh)
+        return rcopy(
+            og_ref.at[:, half_cols(h)],
+            ogb.at[zi_own, s, yh],
+            ys.at[i],
+            yr.at[s, yh],
+            tp=(1 - y if far else y) * 8 + z,
+            sg=target,
+        )
+
+    ysend = [
+        y_send(0, next_to, False),
+        y_send(1, 1 - next_to, False),
+        y_send(2, jnp.where(in_pair, next_to, 1 - next_to), True),
+        y_send(3, jnp.where(in_pair, 1 - next_to, next_to), True),
+    ]
+    other = jnp.logical_not(in_pair)
+    ysend[0].start()
+    pl.when(other)(ysend[1].start)
 
     og_mine = og_ref.at[:, half_cols(lax.rem(s, 2))]
     og_local = pltpu.make_async_copy(og_mine, ogb.at[zi_own, s, yh], lin.at[4])
 
-    pieces = [(s, yh)]
-    for k in range(3):
-        nearer = jnp.where(jnp.abs(seg_at(k) - s) == 3, 1 - yh, yh)
-        pieces += [(seg_at(k), nearer), (seg_at(k), 1 - nearer)]
-    pieces.append((s, 1 - yh))
+    nearer = [jnp.where(jnp.abs(seg_at(k) - s) == 3, 1 - yh, yh) for k in range(3)]
+    pieces = [(s, yh), (seg_at(0), nearer[0]), (seg_at(2), nearer[2]), (seg_at(0), 1 - nearer[0])]
+    pieces += [(seg_at(1), nearer[1]), (seg_at(1), 1 - nearer[1]), (seg_at(2), 1 - nearer[2]), (s, 1 - yh)]
 
     def zcopy(d, n, sem, step):
         zi = lax.div(lax.rem(z - d + 16, 8), 2)
@@ -145,6 +155,9 @@
     local.append(pltpu.make_async_copy(q_ref.at[:, half_cols(c)], qh.at[c], lin.at[3]))
     for cp in local:
         cp.start()
+    ysend[0].wait_send()
+    ysend[2].start()
+    ysend[3].start()
 
     def kv_copy(a, side, core, xs_, xd, rows=None, hop=0):
         blk = kv.at[a, xs_ * 2 + core]
@@ -198,7 +211,8 @@
             rows = pl.ds(b * 128, 128)
             whi[rows, :], wlo[rows, :] = split(wb[b])
 
-    on_right, on_left = (0, 2, 4, 1, 6, 3, 5, 7), (1, 3, 0, 5, 2, 7, 4, 6)
+    on_right, on_left = (1, 0, 2, 3, 5, 4, 7, 6), (0, 4, 1, 3, 5, 6, 2, 7)
+    long_right = (1, 2, 5, 7)
 
     def pass_near(n, odd):
         right, left = (n, n) if odd else (on_right[n], on_left[n])
@@ -210,7 +224,7 @@
         cp.start()
 
     def pass_far(n):
-        cp = zcopy(3, n, zs.at[n, 2], 1) if n % 2 == 0 else zcopy(5, n, zs.at[n, 2], -1)
+        cp = zcopy(3, n, zs.at[n, 2], 1) if n in long_right else zcopy(5, n, zs.at[n, 2], -1)
         cp.wait_recv()
         cp.start()
 
@@ -236,9 +250,9 @@
 
         @pl.when(odd == 1)
         def _():
-            zcopy(5 if n % 2 == 0 else 3, n, zs.at[n, 2], 1).wait_recv()
-
-    def partial_dot(k):
+            zcopy(5 if n in long_right else 3, n, zs.at[n, 2], 1).wait_recv()
+
+    def og_pairs(k):
         j = seg_at(k)
         for zi in range(4):
             for y in range(2):
@@ -246,15 +260,42 @@
                 cols = pl.ds((y * 4 + zi) * HD, HD)
                 oghi[k, :, cols] = hi
                 oglo[k, :, cols] = lo
+
+    def send_partial(k):
+        return [
+            rcopy(psend.at[k, core], dpart.at[s, c], ds.at[k, core], dr.at[s, c], sg=seg_at(k), sq=x * 2 + core)
+            for core in range(2)
+        ]
+
+    def relay():
+        return rcopy(psend.at[0], relayed, ds.at[3, 0], rel_r, sg=jnp.where(s < 2, 1, 2))
+
+    def partial_dot(k):
         res = dot3((oghi[k], oglo[k]), (whi[...], wlo[...]), NN)
         psend[k, 0] = res[:, :HD]
         psend[k, 1] = res[:, HD:]
-        if k < 3:
-            for core in range(2):
-                go(rcopy(psend.at[k, core], dpart.at[k, c], ds.at[k, core], dr.at[k, c], sg=j, sq=x * 2 + core))
+        if k == 0:
+            pl.when(jnp.logical_not(inner))(relay().start)
+
+            @pl.when(inner)
+            def _():
+                for cp in send_partial(0):
+                    cp.start()
+        elif k < 3:
+            if k == 2:
+                @pl.when(inner)
+                def _():
+                    rcopy(relayed, relayed, ds.at[3, 0], rel_r, sg=s, sq=q_sib).wait_recv()
+                    psend[2] = psend[2] + relayed[...]
+            for cp in send_partial(k):
+                go(cp)
         else:
-            go(rcopy(psend.at[3, 1 - c], dpart.at[3, c], ds.at[3, 0], dr.at[3, c], sq=q_sib))
-            dpart[3, c] = psend[3, c]
+            go(rcopy(psend.at[3, 1 - c], dpart.at[s, c], ds.at[3, 1], dr.at[s, c], sq=q_sib))
+            dpart[s, c] = psend[3, c]
+
+            @pl.when(jnp.logical_not(inner))
+            def _():
+                dpart[3 - s] = jnp.zeros((2, 128, HD), F32)
 
     def probs():
         rcopy(qh.at[1 - c], qh.at[1 - c], qs_s, qs_r, sq=q_sib).wait_recv()
@@ -269,7 +310,6 @@
         phi[...], plo[...] = split(p)
 
     ends = (None, s == 3, s == 0)
-    inner = jnp.logical_and(s > 0, s < 3)
     far_seg = jnp.where(s == 2, 0, 3)
     tsends, tnear = [], []
 
@@ -295,7 +335,7 @@
         dqs[...] = res.reshape(2, 128, HD)
         for k in range(3):
             for core in range(2):
-                cp = rcopy(dqs.at[core], att.at[s, c], ts.at[k, core], tr.at[k, c], sg=seg_at(k), sq=x * 2 + core)
+                cp = rcopy(dqs.at[core], att.at[s, c], ts.at[k, core], tr.at[k, c], sg=att_seg(k), sq=x * 2 + core)
                 if k == 0:
                     to(cp)
                 else:
@@ -304,9 +344,9 @@
         to(rcopy(dqs.at[1 - c], att.at[s, c], ts.at[3, 0], tr.at[3, c], sq=q_sib))
         att[s, c] = dqs[c]
 
-    def att_pairs(k):
-        j = seg_at(k)
-        if k < 3:
+    def att_arrived():
+        for k in range(3):
+            j = att_seg(k)
             k_from = (0, 2, 1)[k]
 
             def direct():
@@ -319,9 +359,11 @@
             else:
                 pl.when(jnp.logical_not(ends[k]))(direct)
                 pl.when(ends[k])(att_hop(j, s).wait_recv)
-        else:
-            blk = att.at[s, 1 - c]
-            rcopy(blk, blk, ts.at[3, 0], tr.at[3, 1 - c], sq=q_sib).wait_recv()
+        blk = att.at[s, 1 - c]
+        rcopy(blk, blk, ts.at[3, 0], tr.at[3, 1 - c], sq=q_sib).wait_recv()
+
+    def att_pairs(k):
+        j = seg_at(k)
         for head in range(2):
             cols = pl.ds(head * HD, HD)
             ahi[k, :, cols], alo[k, :, cols] = split(att[j, head])
@@ -339,12 +381,12 @@
 
     ring_steps(owns=(1,), near_odd=(0,))
     kv_near(0)
-    ring_steps(owns=(2, 3, 4), near_odd=(1,))
+    ring_steps(owns=(2, 4, 3), near_odd=(1,))
     kv_near(1)
     w_start()
     ring_steps(owns=(5, 6), near_odd=(2,))
     probs()
-    ring_steps(owns=(7,), near_odd=(3, 4))
+    ring_steps(owns=(7,), near_odd=(4, 3))
     attend()
     ring_steps(near_even=(0,), near_odd=(5,))
     w_near()
@@ -352,20 +394,24 @@
     w_far()
     ring_steps(near_even=(4,), fars=(0,))
     w_done()
-    ring_steps(near_even=(5, 6, 7), fars=(1, 2, 3))
+    ring_steps(near_even=(5, 6, 7), fars=(1, 2, 4))
     att_forward()
-    ring_steps(fars=(4,))
+    ring_steps(fars=(3,))
     arrived(1)
-    arrived(2)
+    arrived(3)
+    og_pairs(0)
     partial_dot(0)
     ring_steps(fars=(5,))
-    arrived(3)
     arrived(4)
+    arrived(5)
+    og_pairs(1)
     partial_dot(1)
     ring_steps(fars=(6, 7))
-    arrived(5)
+    arrived(2)
     arrived(6)
+    og_pairs(2)
     partial_dot(2)
+    att_arrived()
     dw_add(0)
 
     @pl.when(odd == 0)
@@ -374,9 +420,10 @@
 
     arrived(0)
     arrived(7)
-    partial_dot(3)
+    og_pairs(3)
     dw_add(2)
     go(rcopy(wpart.at[:, 1 - c], wsib, ws1, wr1, sq=q_sib))
+    partial_dot(3)
 
     def dw_far():
         rcopy(wpart.at[:, 1 - c], wsib, ws1, wr1, sq=q_sib).wait_recv()
@@ -408,12 +455,19 @@
             go(rcopy(part.at[a, xd, core, rows], near_in.at[a, side, c, rows],
                      fs.at[a, side, stage, core], fr.at[a, side, stage, c], sq=xd * 2 + core))
 
-    def sum_start(a, val):
-        part[a] = val.reshape(4, 2, 128, HD)
+    def sum_start(a, right):
+        def rows_of(xo):
+            rows = pl.ds(pl.multiple_of(xo * 256, 256), 256)
+            part[a, xo] = dot3((phi[rows, :], plo[rows, :]), right, NN).reshape(2, 128, HD)
+
+        rows_of(x_far)
         go(rcopy(part.at[a, x_far, :, up], half.at[a, 0], hs.at[a, 0], hr.at[a, 0], sq=q_right))
         go(rcopy(part.at[a, x_far, :, low], half.at[a, 1], hs.at[a, 1], hr.at[a, 1], sq=q_left))
+        rows_of(x_right)
         near_rows(a, 0, 0, x_right, low)
+        rows_of(x_left)
         near_rows(a, 1, 0, x_left, up)
+        rows_of(x)
         go(rcopy(part.at[a, x, 1 - c], own_in.at[a], os.at[a], orr.at[a], sq=q_sib))
 
     def sum_near(a):
@@ -438,20 +492,24 @@
         outs[a][:, half_cols(1 - c)] = own_in[a] + (near_in[a, 0, 1 - c] + near_in[a, 1, 1 - c])
 
     dw_far()
-    for k in range(3):
-        for core in range(2):
-            blk = dpart.at[k, core]
-            rcopy(blk, blk, ds.at[k, 0], dr.at[k, core], sq=q_sib).wait_recv()
-    blk = dpart.at[3, 1 - c]
-    rcopy(blk, blk, ds.at[3, 0], dr.at[3, 1 - c], sq=q_sib).wait_recv()
+    for d in range(1, 4):
+        src = lax.rem(s + d, 4)
+
+        @pl.when(jnp.logical_or(inner, src != 3 - s))
+        def _():
+            for core in range(2):
+                blk = dpart.at[src, core]
+                rcopy(blk, blk, ds.at[0, 0], dr.at[src, core], sq=q_sib).wait_recv()
+    blk = dpart.at[s, 1 - c]
+    rcopy(blk, blk, ds.at[3, 1], dr.at[s, 1 - c], sq=q_sib).wait_recv()
     datt = ((dpart[0] + dpart[1]) + (dpart[2] + dpart[3])).reshape(256, HD)
     dsp = split(datt)
-    sum_start(1, dot3((phi[...], plo[...]), dsp, NN))
+    sum_start(1, dsp)
     dp = dot3((vhi[...], vlo[...]), dsp, NT)
     p = pt[...]
     dsc = p * (dp - jnp.sum(p * dp, axis=0, keepdims=True))
     phi[...], plo[...] = split(dsc)
-    sum_start(0, dot3((phi[...], plo[...]), (qhi[...], qlo[...]), NN))
+    sum_start(0, (qhi[...], qlo[...]))
     dw_near()
     sum_near(1)
     for cp in tsends:
@@ -471,9 +529,16 @@
 
     for cp in sends:
         cp.wait_send()
-    for i in (0, 1, 3):
-        ysend[i].wait_send()
-    pl.when(other)(ysend[2].wait_send)
+    pl.when(jnp.logical_not(inner))(relay().wait_send)
+
+    @pl.when(inner)
+    def _():
+        for cp in send_partial(0):
+            cp.wait_send()
+
+    pl.when(other)(ysend[1].wait_send)
+    ysend[2].wait_send()
+    ysend[3].wait_send()
 
     @pl.when(odd == 0)
     def _():
@@ -524,6 +589,7 @@
             f32(4, 2, 128, 128),
             f32(4, 2, 128, 128),
             f32(2, 128, 128),
+            f32(2, 128, 128),
             f32(4, 2, 256, 128),
             f32(4, 256, 128),
             f32(4, 256, 128),
@@ -544,7 +610,7 @@
             sem(4), sem(4), sem(4), sem(4),
             sem(4), sem(4, 2),
             sem(8, 3), sem(8, 2), sem(8, 4),
-            sem(4, 2), sem(4, 2), one, one, sem(4, 2), sem(4, 2),
+            sem(4, 2), sem(4, 2), one, one, sem(4, 2), sem(4, 2), one,
             one, one, sem(6), sem(6),
             sem(2, 2), sem(2, 2),
             sem(2, 2, 2, 2), sem(2, 2, 2, 2),

time: 75.1 us -> 71.6 us (0.953)
  Pallas kernels: 74.3 us -> 70.8 us
    pallas_call x1, Pallas kernels: 72.4 us -> 68.9 us  [shards(): pl.pallas_call(body, out_shape=[jax.ShapeDtypeStruct(blk, F32)] * 4, in_s...]
where the time goes in v4:
time: 71.6 us; the launch traced here: 71.5 us
  Pallas kernels  70.8 us (99%)
    pallas_call x1, Pallas kernels, shards(): pl.pallas_call(body, out_shape=[jax.ShapeDtypeStruct(blk, F32)] * 4, in_s...  68.9 us
    pallas_call x1, Pallas kernels, shards(): pl.pallas_call(keep, out_shape=[jax.ShapeDtypeStruct(blk, F32)] * 4, in_s...  1.91 us

profile of v4, /device:TPU:1, one launch (start us, length us, event | category | flops | bytes accessed | tf_op | source)
XLA Modules:
  0.0 71.5 jit_solution(12200331264494592141)
XLA Ops:
  0.6 68.9 %shard_map.84 = (f32[128,256]{1,0:T(8,128)}, f32[128,256]{1,0:T(8,128)}, f32[128,256]{1,0:T(8,128)}, f32[128,256]{1,0:T(8,128)}) custom-call(f32[128,256]{1,0:T(8,128)} %bitcast.7, f32[128,256]{1,0:T(8,128)} %bitcast.8, f32[128,256]{1,0:T(8,128)} %bitcast.9, f32[128,256]{1,0:T(8,128)} %bitcast.10, f32[128,256]{1,0:T(8,128)} %w_ref.1), custom_call_target="tpu_custom_call" | custom-call | flops 2820000000 | bytes 1200000 | tf_op jit(solution)/shard_map/pallas_call | solution.py:576
  69.6 1.9 %shard_map.85 = (f32[128,256]{1,0:T(8,128)}, f32[128,256]{1,0:T(8,128)}, f32[128,256]{1,0:T(8,128)}, f32[128,256]{1,0:T(8,128)}) custom-call(f32[128,256]{1,0:T(8,128)} %get-tuple-element.12.refs_0_, f32[128,256]{1,0:T(8,128)} %get-tuple-element.13.refs_1_, f32[128,256]{1,0:T(8,128)} %get-tuple-element.14.refs_2_, f32[128,256]{1,0:T(8,128)} %get-tuple-element.15.refs_3_), custom_call_target="tpu_custom_call" | custom-call | tf_op jit(solution)/shard_map/pallas_call | solution.py:626

commit v5 on v4

--- a/solution.py
+++ b/solution.py
@@ -38,11 +38,12 @@
 
 def body(
     q_ref, k_ref, v_ref, og_ref, w_ref,
+    dq_out, dk_out, dv_out, dw_out,
     dq_ref, dk_ref, dv_ref, dw_ref,
     qh, kv, wb, ogb, oghi, oglo, att, ahi, alo, psend, dpart, relayed, dqs,
     wpart, wsib, wred, whalf, wfull, part, half, near_in, own_in,
     qhi, qlo, khi, klo, vhi, vlo, whi, wlo, pt, phi, plo,
-    lin, qs_s, qs_r, kxs, kxr, kss, ksr, xs, xr, ss, sr, ys, yr, zs, zo, zr,
+    lout, lin, qs_s, qs_r, kxs, kxr, kss, ksr, xs, xr, ss, sr, ys, yr, zs, zo, zr,
     ts, tr, tf_s, tf_r, ds, dr, rel_r, ws1, wr1, ws2, wr2, hs, hr, fs, fr, os, orr, qos, qor,
 ):
     t = lax.axis_index("tp")
@@ -367,6 +368,9 @@
         for head in range(2):
             cols = pl.ds(head * HD, HD)
             ahi[k, :, cols], alo[k, :, cols] = split(att[j, head])
+
+    def dw_swap(i, xo):
+        return rcopy(wpart.at[xo, 1 - c], wsib.at[xo], ws1.at[i], wr1.at[i], sq=q_sib)
 
     def dw_add(k):
         att_pairs(k)
@@ -422,18 +426,22 @@
     arrived(7)
     og_pairs(3)
     dw_add(2)
-    go(rcopy(wpart.at[:, 1 - c], wsib, ws1, wr1, sq=q_sib))
+    for i, xo in enumerate((x_far, x_right, x_left, x)):
+        go(dw_swap(i, xo))
     partial_dot(3)
 
     def dw_far():
-        rcopy(wpart.at[:, 1 - c], wsib, ws1, wr1, sq=q_sib).wait_recv()
+        dw_swap(0, x_far).wait_recv()
         wred[x_far] = wpart[x_far, c] + wsib[x_far]
         go(rcopy(wred.at[x_far, wup], whalf.at[0], ws2.at[0], wr2.at[0], sq=q_right))
         go(rcopy(wred.at[x_far, wlow], whalf.at[1], ws2.at[1], wr2.at[1], sq=q_left))
+        dw_swap(1, x_right).wait_recv()
         wred[x_right] = wpart[x_right, c] + wsib[x_right]
         go(rcopy(wred.at[x_right, wlow], wfull.at[0, wlow], ws2.at[2], wr2.at[2], sq=q_right))
+        dw_swap(2, x_left).wait_recv()
         wred[x_left] = wpart[x_left, c] + wsib[x_left]
         go(rcopy(wred.at[x_left, wup], wfull.at[1, wup], ws2.at[3], wr2.at[3], sq=q_left))
+        dw_swap(3, x).wait_recv()
         wred[x] = wpart[x, c] + wsib[x]
 
     def dw_near():
@@ -522,10 +530,18 @@
     go(rcopy(dqs.at[1 - c], dq_ref.at[:, half_cols(c)], qos, qor, sq=q_sib))
     dq_ref[:, half_cols(c)] = dqs[c]
     sum_near(0)
+    results = [
+        pltpu.make_async_copy(a, b, lout.at[i])
+        for i, (a, b) in enumerate(((dq_ref, dq_out), (dk_ref, dk_out), (dv_ref, dv_out), (dw_ref, dw_out)))
+    ]
     dw_end()
+    results[3].start()
     sum_end(1)
+    results[2].start()
+    rcopy(dqs.at[1 - c], dq_ref.at[:, half_cols(1 - c)], qos, qor, sq=q_sib).wait_recv()
+    results[0].start()
     sum_end(0)
-    rcopy(dqs.at[1 - c], dq_ref.at[:, half_cols(1 - c)], qos, qor, sq=q_sib).wait_recv()
+    results[1].start()
 
     for cp in sends:
         cp.wait_send()
@@ -536,6 +552,8 @@
         for cp in send_partial(0):
             cp.wait_send()
 
+    for cp in results:
+        cp.wait()
     pl.when(other)(ysend[1].wait_send)
     ysend[2].wait_send()
     ysend[3].wait_send()
@@ -557,11 +575,17 @@
 
 
 def keep(*refs):
-    sems = refs[8]
-    copies = [pltpu.make_async_copy(refs[i], refs[4 + i], sems.at[i]) for i in range(4)]
-    for cp in copies:
+    held, in_sems, out_sems = refs[8:]
+    rows = 128 // 4
+    places = [(i, pl.ds(r * rows, rows)) for r in range(4) for i in range(4)]
+    ins = [pltpu.make_async_copy(refs[i].at[r], held.at[i, r], in_sems.at[n]) for n, (i, r) in enumerate(places)]
+    outs = [pltpu.make_async_copy(held.at[i, r], refs[4 + i].at[r], out_sems.at[n]) for n, (i, r) in enumerate(places)]
+    for cp in ins:
         cp.start()
-    for cp in copies:
+    for arriving, leaving in zip(ins, outs):
+        arriving.wait()
+        leaving.start()
+    for cp in outs:
         cp.wait()
 
 
@@ -577,8 +601,9 @@
         body,
         out_shape=[jax.ShapeDtypeStruct(blk, F32)] * 4,
         in_specs=[hbm] * 5,
-        out_specs=[vmem] * 4,
+        out_specs=[hbm] * 4,
         scratch_shapes=[
+            f32(128, 256), f32(128, 256), f32(128, 256), f32(128, 256),
             f32(2, 128, 128),
             f32(2, 8, 128, 128),
             f32(8, 128, 256),
@@ -605,13 +630,13 @@
             b16(1024, 256), b16(1024, 256),
             f32(1024, 256),
             b16(1024, 256), b16(1024, 256),
-            sem(5), one, one,
+            sem(4), sem(5), one, one,
             sem(2, 4, 2), sem(2, 4, 2), sem(2), sem(2),
             sem(4), sem(4), sem(4), sem(4),
             sem(4), sem(4, 2),
             sem(8, 3), sem(8, 2), sem(8, 4),
             sem(4, 2), sem(4, 2), one, one, sem(4, 2), sem(4, 2), one,
-            one, one, sem(6), sem(6),
+            sem(4), sem(4), sem(6), sem(6),
             sem(2, 2), sem(2, 2),
             sem(2, 2, 2, 2), sem(2, 2, 2, 2),
             sem(2), sem(2), one, one,
@@ -626,9 +651,9 @@
     dq, dk, dv, dw = pl.pallas_call(
         keep,
         out_shape=[jax.ShapeDtypeStruct(blk, F32)] * 4,
-        in_specs=[vmem] * 4,
+        in_specs=[hbm] * 4,
         out_specs=[hbm] * 4,
-        scratch_shapes=[sem(4)],
+        scratch_shapes=[f32(4, 128, 256), sem(16), sem(16)],
         compiler_params=pltpu.CompilerParams(vmem_limit_bytes=60 * 1024 * 1024),
     )(*outs)
     return dq[None], dk[None], dv[None], dw

time: 71.6 us -> 71.5 us (level)
  no operation moved by 1% of the time
where the time goes in v5:
time: 71.5 us; the launch traced here: 71.3 us
  Pallas kernels  70.7 us (99%)
    pallas_call x1, Pallas kernels, shards(): pl.pallas_call(body, out_shape=[jax.ShapeDtypeStruct(blk, F32)] * 4, in_s...  68.8 us
    pallas_call x1, Pallas kernels, shards(): pl.pallas_call(keep, out_shape=[jax.ShapeDtypeStruct(blk, F32)] * 4, in_s...  1.9 us

profile of v5, /device:TPU:1, one launch (start us, length us, event | category | flops | bytes accessed | tf_op | source)
XLA Modules:
  0.0 71.3 jit_solution(4012847218645854677)
XLA Ops:
  0.6 68.8 %shard_map.84 = (f32[128,256]{1,0:T(8,128)}, f32[128,256]{1,0:T(8,128)}, f32[128,256]{1,0:T(8,128)}, f32[128,256]{1,0:T(8,128)}) custom-call(f32[128,256]{1,0:T(8,128)} %bitcast.7, f32[128,256]{1,0:T(8,128)} %bitcast.8, f32[128,256]{1,0:T(8,128)} %bitcast.9, f32[128,256]{1,0:T(8,128)} %bitcast.10, f32[128,256]{1,0:T(8,128)} %w_ref.1), custom_call_target="tpu_custom_call" | custom-call | flops 2820000000 | bytes 1200000 | tf_op jit(solution)/shard_map/pallas_call | solution.py:600
  69.4 1.9 %shard_map.85 = (f32[128,256]{1,0:T(8,128)}, f32[128,256]{1,0:T(8,128)}, f32[128,256]{1,0:T(8,128)}, f32[128,256]{1,0:T(8,128)}) custom-call(f32[128,256]{1,0:T(8,128)} %get-tuple-element.12.refs_0_, f32[128,256]{1,0:T(8,128)} %get-tuple-element.13.refs_1_, f32[128,256]{1,0:T(8,128)} %get-tuple-element.14.refs_2_, f32[128,256]{1,0:T(8,128)} %get-tuple-element.15.refs_3_), custom_call_target="tpu_custom_call" | custom-call | tf_op jit(solution)/shard_map/pallas_call | solution.py:651
